TPU v7x, 512 devices: a whole 4x4x16 slice. The times are simulated.
512 devices in a mesh: gx: 32 (over x, y, z_hi), gy: 16 (over z_lo, core).
Axes of the slice: x: 4, y: 4, z: 16 (z_hi: 2, z_lo: 8; z = z_hi * 8 + z_lo), core: 2. Of those that a mesh axis runs over, the one named last changes fastest.
Arguments:
- sea_level: float32 [4096, 12288], P('gy', 'gx'), may hold values from -6 to 6
- transport_u: float32 [4096, 12288], P('gy', 'gx'), may hold values from -6 to 6
- transport_v: float32 [4096, 12288], P('gy', 'gx'), may hold values from -6 to 6
- ocean_depth: float32 [4096, 12288], P('gy', 'gx'), may hold values from 0.5 to 2
- tracers: float32 [2, 4096, 12288], P(None, 'gy', 'gx'), may hold values from -6 to 6
- land_mask: int32 [4096, 12288], P('gy', 'gx'), may hold values 0 or 1
Outputs:
- new_level: float32 [4096, 12288], P('gy', 'gx')
- new_east_flow: float32 [4096, 12288], P('gy', 'gx')
- new_north_flow: float32 [4096, 12288], P('gy', 'gx')
- new_tracers: float32 [2, 4096, 12288], P(None, 'gy', 'gx')
All inputs are finite; a program needn't handle non-finite values. No bound on the sum of `land_mask` on one device may be relied on, other than what follows from the above.
Results may differ from a plain program's by a relative error of at most 0.00002.
Values sent between devices are 32-bit elements; how exact they have to be, the bound alone decides.
A program may use at most 64 MiB of HBM per device.

v0:
```python
import jax
import jax.numpy as jnp
from jax import lax
from jax.sharding import PartitionSpec as P

SUBSTEPS = 3


DIVERGENCE_STEP = 0.3
GRAVITY_STEP = 0.3
DRAG_RATE = 0.05
CORIOLIS_TOP = 0.4
ADVECT_STEP = 0.1


def from_behind(value, axis, steps):
    count = lax.axis_size(axis)
    pairs = [(source, (source + steps) % count) for source in range(count)]
    return lax.ppermute(value, axis, pairs)


def shifted(value, axis, steps):
    count = lax.axis_size(axis)
    initial, last = (max(0, -steps), min(count, count - steps))
    return lax.ppermute(value, axis, [(source, source + steps) for source in range(initial, last)])


def swapped(value, axis, distance):
    mask = 2**distance
    pairs = [(source, source ^ mask) for source in range(lax.axis_size(axis))]
    return lax.ppermute(value, axis, pairs)


def take_west(field):
    return from_behind(field[..., -1:], "gx", 1)


def take_east(field):
    return from_behind(field[..., :1], "gx", -1)


def take_south(field):
    return shifted(field[..., -1:, :], "gy", 1)


def take_north(field):
    return shifted(field[..., :1, :], "gy", -1)


def mirror_rows(top_rows):
    bit_total = lax.axis_size("gx").bit_length() - 1
    bit_order = list(range(bit_total))
    partner = top_rows
    for bit_number in bit_order:
        partner = swapped(partner, "gx", bit_number)
    return partner[:, ::-1]


def local(sea_level, transport_u, transport_v, ocean_depth, tracers, land_mask):
    row_count = sea_level.shape[0]
    at_top = lax.axis_index("gy") == lax.axis_size("gy") - 1
    total_rows = row_count * lax.axis_size("gy")
    sea_mask = land_mask.astype(jnp.float32)
    static = jnp.stack([ocean_depth, sea_mask])
    static_east = take_east(static)
    static_north = take_north(static)
    static_fold = mirror_rows(static[:, -1, :])
    static_north = jnp.where(at_top, static_fold[:, None, :], static_north)
    depth_east = jnp.concatenate([ocean_depth[:, 1:], static_east[0]], axis=1)
    mask_east = jnp.concatenate([sea_mask[:, 1:], static_east[1]], axis=1)
    depth_north = jnp.concatenate([ocean_depth[1:], static_north[0]], axis=0)
    mask_north = jnp.concatenate([sea_mask[1:], static_north[1]], axis=0)
    east_mask = sea_mask * mask_east
    north_mask = sea_mask * mask_north
    depth_u = 0.5 * (ocean_depth + depth_east)
    depth_v = 0.5 * (ocean_depth + depth_north)
    row_index = (lax.axis_index("gy") * row_count + lax.iota(jnp.int32, row_count)).astype(
        jnp.float32
    )
    coriolis_u = (CORIOLIS_TOP * ((row_index + 0.5) / total_rows))[:, None]
    coriolis_v = (CORIOLIS_TOP * ((row_index + 1.0) / total_rows))[:, None]
    east_flow = east_mask * transport_u
    north_flow = north_mask * transport_v
    level = sea_level
    sum_east = jnp.zeros_like(east_flow)
    sum_north = jnp.zeros_like(north_flow)
    for substep in range(SUBSTEPS):
        west_column = take_west(east_flow)
        flow_west = jnp.concatenate([west_column, east_flow[:, :-1]], axis=1)
        pair_sum = flow_west + east_flow
        folded = mirror_rows(jnp.stack([north_flow[-1], pair_sum[-1]]))
        top_flow = jnp.where(at_top, 0.5 * (north_flow[-1] - folded[0]), north_flow[-1])
        north_sym = jnp.concatenate([north_flow[:-1], top_flow[None]], axis=0)
        south_row = take_south(north_sym)
        with_south = jnp.concatenate([south_row, north_sym], axis=0)
        east_column = take_east(with_south)
        sym_south = with_south[:-1]
        sym_east = jnp.concatenate([north_sym[:, 1:], east_column[1:]], axis=1)
        south_east = jnp.concatenate([sym_south[:, 1:], east_column[:-1]], axis=1)
        pair_north = take_north(pair_sum)
        pair_north = jnp.where(at_top, -folded[1][None], pair_north)
        pair_above = jnp.concatenate([pair_sum[1:], pair_north], axis=0)
        level = level - DIVERGENCE_STEP * sea_mask * (east_flow - flow_west + north_sym - sym_south)
        level_column = take_east(level)
        level_north = take_north(level)
        level_fold = mirror_rows(level[-1:])
        level_north = jnp.where(at_top, level_fold, level_north)
        level_east = jnp.concatenate([level[:, 1:], level_column], axis=1)
        level_above = jnp.concatenate([level[1:], level_north], axis=0)
        mean_v = 0.25 * (north_sym + sym_east + sym_south + south_east)
        mean_u = 0.25 * (pair_sum + pair_above)
        new_east = east_mask * (
            (1.0 - DRAG_RATE / depth_u) * east_flow
            - GRAVITY_STEP * depth_u * (level_east - level)
            + coriolis_u * mean_v
        )
        north_flow = north_mask * (
            (1.0 - DRAG_RATE / depth_v) * north_sym
            - GRAVITY_STEP * depth_v * (level_above - level)
            - coriolis_v * mean_u
        )
        east_flow = new_east
        sum_east = sum_east + east_flow
        sum_north = sum_north + north_flow
    mean_east = sum_east / SUBSTEPS
    mean_plain = sum_north / SUBSTEPS
    folded = mirror_rows(jnp.concatenate([mean_plain[-1:], tracers[:, -1, :]], axis=0))
    top_mean = jnp.where(at_top, 0.5 * (mean_plain[-1] - folded[0]), mean_plain[-1])
    mean_north = jnp.concatenate([mean_plain[:-1], top_mean[None]], axis=0)
    tracer_column = take_east(tracers)
    tracer_north = take_north(tracers)
    tracer_north = jnp.where(at_top, folded[1:, None, :], tracer_north)
    tracer_east = jnp.concatenate([tracers[:, :, 1:], tracer_column], axis=2)
    tracer_above = jnp.concatenate([tracers[:, 1:], tracer_north], axis=1)
    flux_east = jnp.maximum(mean_east, 0.0) * tracers + jnp.minimum(mean_east, 0.0) * tracer_east
    flux_north = (
        jnp.maximum(mean_north, 0.0) * tracers + jnp.minimum(mean_north, 0.0) * tracer_above
    )
    edge_west = take_west(flux_east)
    edge_south = take_south(flux_north)
    flux_west = jnp.concatenate([edge_west, flux_east[:, :, :-1]], axis=2)
    flux_south = jnp.concatenate([edge_south, flux_north[:, :-1]], axis=1)
    change = flux_east - flux_west + flux_north - flux_south
    new_tracers = tracers - ADVECT_STEP * sea_mask * change / ocean_depth
    return (level, east_flow, north_flow, new_tracers)


def solution(mesh):
    return jax.shard_map(
        local,
        mesh=mesh,
        in_specs=(
            P("gy", "gx"),
            P("gy", "gx"),
            P("gy", "gx"),
            P("gy", "gx"),
            P(None, "gy", "gx"),
            P("gy", "gx"),
        ),
        out_specs=(P("gy", "gx"), P("gy", "gx"), P("gy", "gx"), P(None, "gy", "gx")),
        check_vma=False,
    )
```

profile of v0, /device:TPU:1, one launch (start us, length us, event | category | flops | bytes accessed | tf_op | source)
XLA Modules:
  0.0 532.7 jit_solution(5656356131481070104)
XLA Ops:
  2.9 16.3 %collective-permute-start.2 = (f32[2,384]{1,0:T(2,128)S(1)}, f32[2,384]{1,0:T(2,128)S(1)}, u32[]{:S(2)}, u32[]{:S(2)}) collective-permute-start(f32[2,384]{1,0:T(2,128)S(1)} %get-tuple-element.20), channel_id=1, source_target_pairs={{0,16},{16,0},{32,48},{48,32},{64,80},{80,64},{96,112},{112,96},{1... | collective-permute-start | bytes 9224 | tf_op jit(solution)/shard_map/ppermute | solution.py:31
  33.7 16.1 %collective-permute-start = (f32[2,256,1]{2,0,1:T(2,128)S(1)}, f32[2,256,1]{2,0,1:T(2,128)S(1)}, u32[]{:S(2)}, u32[]{:S(2)}) collective-permute-start(f32[2,256,1]{2,0,1:T(2,128)S(1)} %fusion.51), channel_id=1, source_target_pairs={{0,496},{16,0},{32,16},{48,32},{64,48},{80,64},{96,80},{112,96},{1... | collective-permute-start | bytes 6152 | tf_op jit(solution)/shard_map/ppermute | solution.py:19
  49.8 6.6 %collective-permute-start.7 = (f32[2,1,384]{2,0,1:T(2,128)S(1)}, f32[2,1,384]{2,0,1:T(2,128)S(1)}, u32[]{:S(2)}, u32[]{:S(2)}) collective-permute-start(f32[2,1,384]{2,0,1:T(2,128)S(1)} %get-tuple-element.21), channel_id=1, source_target_pairs={{1,0},{2,1},{3,2},{4,3},{5,4},{6,5},{7,6},{8,7},{9,8},{10,9},{11,1... | collective-permute-start | bytes 9224 | tf_op jit(solution)/shard_map/ppermute | solution.py:25
  63.0 10.9 %collective-permute-done.7 = f32[2,1,384]{2,0,1:T(2,128)S(1)} collective-permute-done((f32[2,1,384]{2,0,1:T(2,128)S(1)}, f32[2,1,384]{2,0,1:T(2,128)S(1)}, u32[]{:S(2)}, u32[]{:S(2)}) %collective-permute-start.7) | collective-permute-done | bytes 3104 | tf_op jit(solution)/shard_map/ppermute | solution.py:25
  77.9 21.1 %collective-permute-done.1 = f32[256,1]{1,0:T(8,128)S(1)} collective-permute-done((f32[256,1]{1,0:T(8,128)S(1)}, f32[256,1]{1,0:T(8,128)S(1)}, u32[]{:S(2)}, u32[]{:S(2)}) %collective-permute-start.1) | collective-permute-done | bytes 1056 | tf_op jit(solution)/shard_map/ppermute | solution.py:19
  102.1 11.1 %collective-permute-done.8 = f32[2,384]{1,0:T(2,128)S(1)} collective-permute-done((f32[2,384]{1,0:T(2,128)S(1)}, f32[2,384]{1,0:T(2,128)S(1)}, u32[]{:S(2)}, u32[]{:S(2)}) %collective-permute-start.8) | collective-permute-done | bytes 3104 | tf_op jit(solution)/shard_map/ppermute | solution.py:31
  133.9 8.0 %collective-permute-start.13 = (f32[1,384]{1,0:T(1,128)S(1)}, f32[1,384]{1,0:T(1,128)S(1)}, u32[]{:S(2)}, u32[]{:S(2)}) collective-permute-start(f32[1,384]{1,0:T(1,128)S(1)} %broadcast_select_fusion.9), channel_id=1, source_target_pairs={{0,1},{1,2},{2,3},{3,4},{4,5},{5,6},{6,7},{7,8},{8,9},{9,10},{10,1... | collective-permute-start | bytes 4616 | tf_op jit(solution)/shard_map/ppermute | solution.py:25
  149.6 11.7 %collective-permute-start.15 = (f32[257,1]{1,0:T(8,128)S(1)}, f32[257,1]{1,0:T(8,128)S(1)}, u32[]{:S(2)}, u32[]{:S(2)}) collective-permute-start(f32[257,1]{1,0:T(8,128)S(1)} %pad_maximum_fusion.14), channel_id=1, source_target_pairs={{0,496},{16,0},{32,16},{48,32},{64,48},{80,64},{96,80},{112,96},{1... | collective-permute-start | bytes 3092 | tf_op jit(solution)/shard_map/ppermute | solution.py:19
  163.3 12.1 %collective-permute-start.17 = (f32[1,384]{1,0:T(1,128)S(1)}, f32[1,384]{1,0:T(1,128)S(1)}, u32[]{:S(2)}, u32[]{:S(2)}) collective-permute-start(f32[1,384]{1,0:T(1,128)S(1)} %get-tuple-element.41), channel_id=1, source_target_pairs={{0,16},{16,0},{32,48},{48,32},{64,80},{80,64},{96,112},{112,96},{1... | collective-permute-start | bytes 4616 | tf_op jit(solution)/shard_map/ppermute | solution.py:31
  181.0 10.5 %collective-permute-start.16 = (f32[256,1]{1,0:T(8,128)S(1)}, f32[256,1]{1,0:T(8,128)S(1)}, u32[]{:S(2)}, u32[]{:S(2)}) collective-permute-start(f32[256,1]{1,0:T(8,128)S(1)} %slice.393), channel_id=1, source_target_pairs={{0,16},{16,32},{32,48},{48,64},{64,80},{80,96},{96,112},{112,128},... | collective-permute-start | bytes 3080 | tf_op jit(solution)/shard_map/ppermute | solution.py:19
  211.8 6.9 %collective-permute-start.24 = (f32[2,384]{1,0:T(2,128)S(1)}, f32[2,384]{1,0:T(2,128)S(1)}, u32[]{:S(2)}, u32[]{:S(2)}) collective-permute-start(f32[2,384]{1,0:T(2,128)S(1)} %pad_maximum_fusion.19), channel_id=1, source_target_pairs={{0,16},{16,0},{32,48},{48,32},{64,80},{80,64},{96,112},{112,96},{1... | collective-permute-start | bytes 9224 | tf_op jit(solution)/shard_map/ppermute | solution.py:31
  218.6 6.2 %collective-permute-done.24 = f32[2,384]{1,0:T(2,128)S(1)} collective-permute-done((f32[2,384]{1,0:T(2,128)S(1)}, f32[2,384]{1,0:T(2,128)S(1)}, u32[]{:S(2)}, u32[]{:S(2)}) %collective-permute-start.24) | collective-permute-done | bytes 3104 | tf_op jit(solution)/shard_map/ppermute | solution.py:31
  247.2 14.7 %collective-permute-start.29 = (f32[1,384]{1,0:T(1,128)S(1)}, f32[1,384]{1,0:T(1,128)S(1)}, u32[]{:S(2)}, u32[]{:S(2)}) collective-permute-start(f32[1,384]{1,0:T(1,128)S(1)} %broadcast_select_fusion.6), channel_id=1, source_target_pairs={{0,1},{1,2},{2,3},{3,4},{4,5},{5,6},{6,7},{7,8},{8,9},{9,10},{10,1... | collective-permute-start | bytes 4616 | tf_op jit(solution)/shard_map/ppermute | solution.py:25
  266.8 11.3 %collective-permute-start.31 = (f32[257,1]{1,0:T(8,128)S(1)}, f32[257,1]{1,0:T(8,128)S(1)}, u32[]{:S(2)}, u32[]{:S(2)}) collective-permute-start(f32[257,1]{1,0:T(8,128)S(1)} %pad_maximum_fusion.12), channel_id=1, source_target_pairs={{0,496},{16,0},{32,16},{48,32},{64,48},{80,64},{96,80},{112,96},{1... | collective-permute-start | bytes 3092 | tf_op jit(solution)/shard_map/ppermute | solution.py:19
  281.7 10.4 %collective-permute-start.33 = (f32[1,384]{1,0:T(1,128)S(1)}, f32[1,384]{1,0:T(1,128)S(1)}, u32[]{:S(2)}, u32[]{:S(2)}) collective-permute-start(f32[1,384]{1,0:T(1,128)S(1)} %get-tuple-element.35), channel_id=1, source_target_pairs={{0,16},{16,0},{32,48},{48,32},{64,80},{80,64},{96,112},{112,96},{1... | collective-permute-start | bytes 4616 | tf_op jit(solution)/shard_map/ppermute | solution.py:31
  292.5 15.0 %collective-permute-done.33 = f32[1,384]{1,0:T(1,128)S(1)} collective-permute-done((f32[1,384]{1,0:T(1,128)S(1)}, f32[1,384]{1,0:T(1,128)S(1)}, u32[]{:S(2)}, u32[]{:S(2)}) %collective-permute-start.33) | collective-permute-done | bytes 1568 | tf_op jit(solution)/shard_map/ppermute | solution.py:31
  323.9 6.9 %collective-permute-done.32 = f32[256,1]{1,0:T(8,128)S(1)} collective-permute-done((f32[256,1]{1,0:T(8,128)S(1)}, f32[256,1]{1,0:T(8,128)S(1)}, u32[]{:S(2)}, u32[]{:S(2)}) %collective-permute-start.32) | collective-permute-done | bytes 1056 | tf_op jit(solution)/shard_map/ppermute | solution.py:19
  343.7 9.0 %collective-permute-done.40 = f32[2,384]{1,0:T(2,128)S(1)} collective-permute-done((f32[2,384]{1,0:T(2,128)S(1)}, f32[2,384]{1,0:T(2,128)S(1)}, u32[]{:S(2)}, u32[]{:S(2)}) %collective-permute-start.40) | collective-permute-done | bytes 3104 | tf_op jit(solution)/shard_map/ppermute | solution.py:31
  381.6 10.1 %collective-permute-start.48 = (f32[1,384]{1,0:T(1,128)S(1)}, f32[1,384]{1,0:T(1,128)S(1)}, u32[]{:S(2)}, u32[]{:S(2)}) collective-permute-start(f32[1,384]{1,0:T(1,128)S(1)} %get-tuple-element.27), channel_id=1, source_target_pairs={{0,16},{16,0},{32,48},{48,32},{64,80},{80,64},{96,112},{112,96},{1... | collective-permute-start | bytes 4616 | tf_op jit(solution)/shard_map/ppermute | solution.py:31
  411.6 13.5 %collective-permute-start.55 = (f32[2,256,1]{2,1,0:T(8,128)}, f32[2,256,1]{2,1,0:T(8,128)}, u32[]{:S(2)}, u32[]{:S(2)}) collective-permute-start(f32[2,256,1]{2,1,0:T(8,128)} %slice.356), channel_id=1, source_target_pairs={{0,496},{16,0},{32,16},{48,32},{64,48},{80,64},{96,80},{112,96},{1... | collective-permute-start | bytes 6152 | tf_op jit(solution)/shard_map/ppermute | solution.py:19
  439.1 15.7 %collective-permute-done.53 = f32[1,384]{1,0:T(1,128)} collective-permute-done((f32[1,384]{1,0:T(1,128)}, f32[1,384]{1,0:T(1,128)}, u32[]{:S(2)}, u32[]{:S(2)}) %collective-permute-start.53) | collective-permute-done | bytes 1568 | tf_op jit(solution)/shard_map/ppermute | solution.py:25
  460.0 12.0 %collective-permute-start.47 = (f32[257,1]{1,0:T(8,128)S(1)}, f32[257,1]{1,0:T(8,128)S(1)}, u32[]{:S(2)}, u32[]{:S(2)}) collective-permute-start(f32[257,1]{1,0:T(8,128)S(1)} %pad_maximum_fusion.10), channel_id=1, source_target_pairs={{0,496},{16,0},{32,16},{48,32},{64,48},{80,64},{96,80},{112,96},{1... | collective-permute-start | bytes 3092 | tf_op jit(solution)/shard_map/ppermute | solution.py:19
  504.7 12.4 %collective-permute-start.56 = (f32[2,256,1]{2,1,0:T(8,128)S(1)}, f32[2,256,1]{2,1,0:T(8,128)S(1)}, u32[]{:S(2)}, u32[]{:S(2)}) collective-permute-start(f32[2,256,1]{2,1,0:T(8,128)S(1)} %slice.440), channel_id=1, source_target_pairs={{0,16},{16,32},{32,48},{48,64},{64,80},{80,96},{96,112},{112,128},... | collective-permute-start | bytes 6152 | tf_op jit(solution)/shard_map/ppermute | solution.py:19
  517.1 14.3 %collective-permute-done.56 = f32[2,256,1]{2,1,0:T(8,128)S(1)} collective-permute-done((f32[2,256,1]{2,1,0:T(8,128)S(1)}, f32[2,256,1]{2,1,0:T(8,128)S(1)}, u32[]{:S(2)}, u32[]{:S(2)}) %collective-permute-start.56) | collective-permute-done | bytes 2080 | tf_op jit(solution)/shard_map/ppermute | solution.py:19
  (284 shorter events, 248.1 us)
Async XLA Ops:
  30.4 26.3 %collective-permute-start.5 = (f32[2,384]{1,0:T(2,128)S(1)}, f32[2,384]{1,0:T(2,128)S(1)}, u32[]{:S(2)}, u32[]{:S(2)}) collective-permute-start(f32[2,384]{1,0:T(2,128)S(1)} %collective-permute-done.4), channel_id=1, source_target_pairs={{0,128},{16,144},{32,160},{48,176},{64,192},{80,208},{96,224},{112... | collective-permute-start | bytes 9224 | tf_op jit(solution)/shard_map/ppermute | solution.py:31
  33.7 25.2 %collective-permute-start = (f32[2,256,1]{2,0,1:T(2,128)S(1)}, f32[2,256,1]{2,0,1:T(2,128)S(1)}, u32[]{:S(2)}, u32[]{:S(2)}) collective-permute-start(f32[2,256,1]{2,0,1:T(2,128)S(1)} %fusion.51), channel_id=1, source_target_pairs={{0,496},{16,0},{32,16},{48,32},{64,48},{80,64},{96,80},{112,96},{1... | collective-permute-start | bytes 6152 | tf_op jit(solution)/shard_map/ppermute | solution.py:19
  49.8 24.2 %collective-permute-start.7 = (f32[2,1,384]{2,0,1:T(2,128)S(1)}, f32[2,1,384]{2,0,1:T(2,128)S(1)}, u32[]{:S(2)}, u32[]{:S(2)}) collective-permute-start(f32[2,1,384]{2,0,1:T(2,128)S(1)} %get-tuple-element.21), channel_id=1, source_target_pairs={{1,0},{2,1},{3,2},{4,3},{5,4},{6,5},{7,6},{8,7},{9,8},{10,9},{11,1... | collective-permute-start | bytes 9224 | tf_op jit(solution)/shard_map/ppermute | solution.py:25
  75.9 23.0 %collective-permute-start.1 = (f32[256,1]{1,0:T(8,128)S(1)}, f32[256,1]{1,0:T(8,128)S(1)}, u32[]{:S(2)}, u32[]{:S(2)}) collective-permute-start(f32[256,1]{1,0:T(8,128)S(1)} %slice.374), channel_id=1, source_target_pairs={{0,16},{16,32},{32,48},{48,64},{64,80},{80,96},{96,112},{112,128},... | collective-permute-start | bytes 3080 | tf_op jit(solution)/shard_map/ppermute | solution.py:19
  143.6 49.9 %collective-permute-start.23 = (f32[1,384]{1,0:T(1,128)}, f32[1,384]{1,0:T(1,128)}, u32[]{:S(2)}, u32[]{:S(2)}) collective-permute-start(f32[1,384]{1,0:T(1,128)} %get-tuple-element.38), channel_id=1, source_target_pairs={{1,0},{2,1},{3,2},{4,3},{5,4},{6,5},{7,6},{8,7},{9,8},{10,9},{11,1... | collective-permute-start | bytes 4616 | tf_op jit(solution)/shard_map/ppermute | solution.py:25
  149.6 26.0 %collective-permute-start.15 = (f32[257,1]{1,0:T(8,128)S(1)}, f32[257,1]{1,0:T(8,128)S(1)}, u32[]{:S(2)}, u32[]{:S(2)}) collective-permute-start(f32[257,1]{1,0:T(8,128)S(1)} %pad_maximum_fusion.14), channel_id=1, source_target_pairs={{0,496},{16,0},{32,16},{48,32},{64,48},{80,64},{96,80},{112,96},{1... | collective-permute-start | bytes 3092 | tf_op jit(solution)/shard_map/ppermute | solution.py:19
  161.3 18.5 %collective-permute-start.14 = (f32[256,1]{1,0:T(8,128)S(1)}, f32[256,1]{1,0:T(8,128)S(1)}, u32[]{:S(2)}, u32[]{:S(2)}) collective-permute-start(f32[256,1]{1,0:T(8,128)S(1)} %slice.386), channel_id=1, source_target_pairs={{0,496},{16,0},{32,16},{48,32},{64,48},{80,64},{96,80},{112,96},{1... | collective-permute-start | bytes 3080 | tf_op jit(solution)/shard_map/ppermute | solution.py:19
  181.0 19.8 %collective-permute-start.16 = (f32[256,1]{1,0:T(8,128)S(1)}, f32[256,1]{1,0:T(8,128)S(1)}, u32[]{:S(2)}, u32[]{:S(2)}) collective-permute-start(f32[256,1]{1,0:T(8,128)S(1)} %slice.393), channel_id=1, source_target_pairs={{0,16},{16,32},{32,48},{48,64},{64,80},{80,96},{96,112},{112,128},... | collective-permute-start | bytes 3080 | tf_op jit(solution)/shard_map/ppermute | solution.py:19
  247.2 18.6 %collective-permute-start.29 = (f32[1,384]{1,0:T(1,128)S(1)}, f32[1,384]{1,0:T(1,128)S(1)}, u32[]{:S(2)}, u32[]{:S(2)}) collective-permute-start(f32[1,384]{1,0:T(1,128)S(1)} %broadcast_select_fusion.6), channel_id=1, source_target_pairs={{0,1},{1,2},{2,3},{3,4},{4,5},{5,6},{6,7},{7,8},{8,9},{9,10},{10,1... | collective-permute-start | bytes 4616 | tf_op jit(solution)/shard_map/ppermute | solution.py:25
  262.7 54.1 %collective-permute-start.39 = (f32[1,384]{1,0:T(1,128)}, f32[1,384]{1,0:T(1,128)}, u32[]{:S(2)}, u32[]{:S(2)}) collective-permute-start(f32[1,384]{1,0:T(1,128)} %get-tuple-element.32), channel_id=1, source_target_pairs={{1,0},{2,1},{3,2},{4,3},{5,4},{6,5},{7,6},{8,7},{9,8},{10,9},{11,1... | collective-permute-start | bytes 4616 | tf_op jit(solution)/shard_map/ppermute | solution.py:25
  266.8 25.6 %collective-permute-start.31 = (f32[257,1]{1,0:T(8,128)S(1)}, f32[257,1]{1,0:T(8,128)S(1)}, u32[]{:S(2)}, u32[]{:S(2)}) collective-permute-start(f32[257,1]{1,0:T(8,128)S(1)} %pad_maximum_fusion.12), channel_id=1, source_target_pairs={{0,496},{16,0},{32,16},{48,32},{64,48},{80,64},{96,80},{112,96},{1... | collective-permute-start | bytes 3092 | tf_op jit(solution)/shard_map/ppermute | solution.py:19
  278.1 31.3 %collective-permute-start.30 = (f32[256,1]{1,0:T(8,128)S(1)}, f32[256,1]{1,0:T(8,128)S(1)}, u32[]{:S(2)}, u32[]{:S(2)}) collective-permute-start(f32[256,1]{1,0:T(8,128)S(1)} %slice.407), channel_id=1, source_target_pairs={{0,496},{16,0},{32,16},{48,32},{64,48},{80,64},{96,80},{112,96},{1... | collective-permute-start | bytes 3080 | tf_op jit(solution)/shard_map/ppermute | solution.py:19
  281.7 25.8 %collective-permute-start.33 = (f32[1,384]{1,0:T(1,128)S(1)}, f32[1,384]{1,0:T(1,128)S(1)}, u32[]{:S(2)}, u32[]{:S(2)}) collective-permute-start(f32[1,384]{1,0:T(1,128)S(1)} %get-tuple-element.35), channel_id=1, source_target_pairs={{0,16},{16,0},{32,48},{48,32},{64,80},{80,64},{96,112},{112,96},{1... | collective-permute-start | bytes 4616 | tf_op jit(solution)/shard_map/ppermute | solution.py:31
  309.9 20.9 %collective-permute-start.32 = (f32[256,1]{1,0:T(8,128)S(1)}, f32[256,1]{1,0:T(8,128)S(1)}, u32[]{:S(2)}, u32[]{:S(2)}) collective-permute-start(f32[256,1]{1,0:T(8,128)S(1)} %slice.414), channel_id=1, source_target_pairs={{0,16},{16,32},{32,48},{48,64},{64,80},{80,96},{96,112},{112,128},... | collective-permute-start | bytes 3080 | tf_op jit(solution)/shard_map/ppermute | solution.py:19
  318.3 19.2 %collective-permute-start.38 = (f32[1,384]{1,0:T(1,128)}, f32[1,384]{1,0:T(1,128)S(1)}, u32[]{:S(2)}, u32[]{:S(2)}) collective-permute-start(f32[1,384]{1,0:T(1,128)} %get-tuple-element.34), channel_id=1, source_target_pairs={{1,0},{2,1},{3,2},{4,3},{5,4},{6,5},{7,6},{8,7},{9,8},{10,9},{11,1... | collective-permute-start | bytes 4616 | tf_op jit(solution)/shard_map/ppermute | solution.py:25
  404.4 28.6 %collective-permute-start.54 = (f32[1,384]{1,0:T(1,128)S(1)}, f32[1,384]{1,0:T(1,128)S(1)}, u32[]{:S(2)}, u32[]{:S(2)}) collective-permute-start(f32[1,384]{1,0:T(1,128)S(1)} %copy-done.36), channel_id=1, source_target_pairs={{1,0},{2,1},{3,2},{4,3},{5,4},{6,5},{7,6},{8,7},{9,8},{10,9},{11,1... | collective-permute-start | bytes 4616 | tf_op jit(solution)/shard_map/ppermute | solution.py:25
  406.3 24.8 %collective-permute-start.51 = (f32[1,384]{1,0:T(1,128)S(1)}, f32[1,384]{1,0:T(1,128)}, u32[]{:S(2)}, u32[]{:S(2)}) collective-permute-start(f32[1,384]{1,0:T(1,128)S(1)} %collective-permute-done.50), channel_id=1, source_target_pairs={{0,128},{16,144},{32,160},{48,176},{64,192},{80,208},{96,224},{112... | collective-permute-start | bytes 4616 | tf_op jit(solution)/shard_map/ppermute | solution.py:31
  409.0 88.7 %collective-permute-start.62 = (f32[2,1,384]{2,0,1:T(2,128)}, f32[2,1,384]{2,0,1:T(2,128)}, u32[]{:S(2)}, u32[]{:S(2)}) collective-permute-start(f32[2,1,384]{2,0,1:T(2,128)} %copy.16), channel_id=1, source_target_pairs={{1,0},{2,1},{3,2},{4,3},{5,4},{6,5},{7,6},{8,7},{9,8},{10,9},{11,1... | collective-permute-start | bytes 9224 | tf_op jit(solution)/shard_map/ppermute | solution.py:25
  411.6 86.8 %collective-permute-start.55 = (f32[2,256,1]{2,1,0:T(8,128)}, f32[2,256,1]{2,1,0:T(8,128)}, u32[]{:S(2)}, u32[]{:S(2)}) collective-permute-start(f32[2,256,1]{2,1,0:T(8,128)} %slice.356), channel_id=1, source_target_pairs={{0,496},{16,0},{32,16},{48,32},{64,48},{80,64},{96,80},{112,96},{1... | collective-permute-start | bytes 6152 | tf_op jit(solution)/shard_map/ppermute | solution.py:19
  429.1 25.7 %collective-permute-start.53 = (f32[1,384]{1,0:T(1,128)}, f32[1,384]{1,0:T(1,128)}, u32[]{:S(2)}, u32[]{:S(2)}) collective-permute-start(f32[1,384]{1,0:T(1,128)} %get-tuple-element.26), channel_id=1, source_target_pairs={{1,0},{2,1},{3,2},{4,3},{5,4},{6,5},{7,6},{8,7},{9,8},{10,9},{11,1... | collective-permute-start | bytes 4616 | tf_op jit(solution)/shard_map/ppermute | solution.py:25
  460.0 23.1 %collective-permute-start.47 = (f32[257,1]{1,0:T(8,128)S(1)}, f32[257,1]{1,0:T(8,128)S(1)}, u32[]{:S(2)}, u32[]{:S(2)}) collective-permute-start(f32[257,1]{1,0:T(8,128)S(1)} %pad_maximum_fusion.10), channel_id=1, source_target_pairs={{0,496},{16,0},{32,16},{48,32},{64,48},{80,64},{96,80},{112,96},{1... | collective-permute-start | bytes 3092 | tf_op jit(solution)/shard_map/ppermute | solution.py:19
  472.0 17.3 %collective-permute-start.46 = (f32[256,1]{1,0:T(8,128)S(1)}, f32[256,1]{1,0:T(8,128)S(1)}, u32[]{:S(2)}, u32[]{:S(2)}) collective-permute-start(f32[256,1]{1,0:T(8,128)S(1)} %slice.427), channel_id=1, source_target_pairs={{0,496},{16,0},{32,16},{48,32},{64,48},{80,64},{96,80},{112,96},{1... | collective-permute-start | bytes 3080 | tf_op jit(solution)/shard_map/ppermute | solution.py:19
  500.9 30.5 %collective-permute-start.63 = (f32[2,1,384]{2,1,0:T(1,128)S(1)}, f32[2,1,384]{2,1,0:T(1,128)S(1)}, u32[]{:S(2)}, u32[]{:S(2)}) collective-permute-start(f32[2,1,384]{2,1,0:T(1,128)S(1)} %slice.446), channel_id=1, source_target_pairs={{0,1},{1,2},{2,3},{3,4},{4,5},{5,6},{6,7},{7,8},{8,9},{9,10},{10,1... | collective-permute-start | bytes 9224 | tf_op jit(solution)/shard_map/ppermute | solution.py:25
  504.7 26.6 %collective-permute-start.56 = (f32[2,256,1]{2,1,0:T(8,128)S(1)}, f32[2,256,1]{2,1,0:T(8,128)S(1)}, u32[]{:S(2)}, u32[]{:S(2)}) collective-permute-start(f32[2,256,1]{2,1,0:T(8,128)S(1)} %slice.440), channel_id=1, source_target_pairs={{0,16},{16,32},{32,48},{48,64},{64,80},{80,96},{96,112},{112,128},... | collective-permute-start | bytes 6152 | tf_op jit(solution)/shard_map/ppermute | solution.py:19
  (77 other events, 1454.8 us)
where the time goes:
time: 543 us; the launch traced here: 533 us
  starting transfers between devices  301 us (55%)
  waiting for transfers between devices  177 us (33%)
  local copies, waits for them, and re-layouts  29.8 us (5%)
  other arithmetic  23 us (4%)
    ppermute x40, starting transfers between devices, swapped(): return lax.ppermute(value, axis, pairs)  147 us
    ppermute x12, starting transfers between devices, from_behind(): return lax.ppermute(value, axis, pairs)  102 us
    ppermute x40, waiting for transfers between devices, swapped(): return lax.ppermute(value, axis, pairs)  100 us
    ppermute x12, starting transfers between devices, shifted(): lax.ppermute(value, axis, [(source, source + steps) for source in range(i...  51.3 us
    ppermute x12, waiting for transfers between devices, from_behind(): return lax.ppermute(value, axis, pairs)  49.5 us
    ppermute x12, waiting for transfers between devices, shifted(): lax.ppermute(value, axis, [(source, source + steps) for source in range(i...  27.4 us
  transfers between devices with their start and end apart: 64, of which 41 were waited for; matrix products, arithmetic and copies ran while one was open for 6% of the time, Pallas kernels for 0%

commit v1 on v0

v1 whole, which is shorter than its diff:
```python
import functools

import jax
import jax.numpy as jnp
from jax import lax
from jax.experimental import pallas as pl
from jax.experimental.pallas import tpu as pltpu
from jax.sharding import PartitionSpec as P

SUBSTEPS = 3
DIVERGENCE_STEP = 0.3
GRAVITY_STEP = 0.3
DRAG_RATE = 0.05
CORIOLIS_TOP = 0.4
ADVECT_STEP = 0.1

MESH = pl.DeviceIdType.MESH
FIELDS = 7
U, V, LEVEL, MASK, DEPTH, T0, T1 = range(FIELDS)
GROUP = 16
BLOCK = 32
W, E, S, N, SW, SE, NW, NE = range(8)


def roll(x, shift, axis):
    return pltpu.roll(x, shift % x.shape[axis], axis)


def lanes(shape):
    return lax.broadcasted_iota(jnp.int32, shape, 1)


def sublanes(shape):
    return lax.broadcasted_iota(jnp.int32, shape, 0)


def advance(u, v, level, mask, depth, tracers, cor_u, cor_v, row_axis, fold=None):
    col_axis = 1 - row_axis
    west = lambda x: roll(x, 1, col_axis)
    east = lambda x: roll(x, -1, col_axis)
    south = lambda x: roll(x, 1, row_axis)
    north = lambda x: roll(x, -1, row_axis)
    head = lambda x: x[:8]

    def sym(x, other):
        return jnp.concatenate([jnp.where(fold[0], 0.5 * (head(x) - other), head(x)), x[8:]], axis=0)

    east_mask = mask * east(mask)
    north_mask = mask * north(mask)
    depth_u = 0.5 * (depth + east(depth))
    depth_v = 0.5 * (depth + north(depth))
    keep_u = east_mask * (1.0 - DRAG_RATE / depth_u)
    keep_v = north_mask * (1.0 - DRAG_RATE / depth_v)
    push_u = east_mask * (GRAVITY_STEP * depth_u)
    push_v = north_mask * (GRAVITY_STEP * depth_v)
    turn_u = east_mask * (0.25 * cor_u)
    turn_v = north_mask * (0.25 * cor_v)
    spread = DIVERGENCE_STEP * mask
    u = east_mask * u
    v = north_mask * v
    if fold is not None:
        other = head(north_mask) * fold[1]
    for step in range(SUBSTEPS):
        if fold is not None:
            v, other = sym(v, other), 0.5 * (other - head(v))
        flow_west = west(u)
        pair = flow_west + u
        sym_south = south(v)
        level = level - spread * (u - flow_west + v - sym_south)
        both = v + sym_south
        pairs = pair + north(pair)
        slope_v = north(level) - level
        new_u = keep_u * u - push_u * (east(level) - level) + turn_u * (both + east(both))
        if fold is not None:
            other = head(keep_v) * other + head(push_v) * head(slope_v) + head(turn_v) * head(pairs)
        v = keep_v * v - push_v * slope_v - turn_v * pairs
        u = new_u
        sum_u = u if step == 0 else sum_u + u
        sum_v = v if step == 0 else sum_v + v
        if fold is not None:
            sum_other = other if step == 0 else sum_other + other
    mean_u = sum_u * (1.0 / SUBSTEPS)
    mean_v = sum_v * (1.0 / SUBSTEPS)
    if fold is not None:
        mean_v = sym(mean_v, sum_other * (1.0 / SUBSTEPS))
    out_u, in_u = jnp.maximum(mean_u, 0.0), jnp.minimum(mean_u, 0.0)
    out_v, in_v = jnp.maximum(mean_v, 0.0), jnp.minimum(mean_v, 0.0)
    rate = ADVECT_STEP * mask / depth
    new = []
    for t in tracers:
        flux_u = out_u * t + in_u * east(t)
        flux_v = out_v * t + in_v * north(t)
        new.append(t - rate * (flux_u - west(flux_u) + flux_v - south(flux_v)))
    return level, u, v, new[0], new[1]


def pack_last(x):
    s = sublanes(x[0].shape)
    return [
        jnp.where(s < 4, roll(x[U], 4, 0), x[V]),
        jnp.where(s < 4, roll(x[LEVEL], 4, 0), x[MASK]),
        jnp.where(s < 4, roll(x[DEPTH], 4, 0), jnp.where(s < 6, roll(x[T0], 6, 0), x[T1])),
    ]


def pack_first(x):
    s = sublanes(x[0].shape)
    return [
        jnp.where(s < 4, x[U], roll(x[V], 4, 0)),
        jnp.where(s < 4, x[LEVEL], roll(x[MASK], 4, 0)),
        jnp.where(s < 4, x[DEPTH], jnp.where(s < 6, roll(x[T0], 4, 0), roll(x[T1], 6, 0))),
    ]


def unpack_last(ref):
    a, b, c = ref[0:8], ref[8:16], ref[16:24]
    return [roll(a, 4, 0), a, roll(b, 4, 0), b, roll(c, 4, 0), roll(c, 2, 0), c]


def unpack_first(ref):
    a, b, c = ref[0:8], ref[8:16], ref[16:24]
    return [a, roll(a, 4, 0), b, roll(b, 4, 0), c, roll(c, 4, 0), roll(c, 2, 0)]


def flip(x, axis, group):
    at = lax.broadcasted_iota(jnp.int32, x.shape, axis)
    bit = 1
    while bit < group:
        x = jnp.where(at & bit == 0, roll(x, -bit, axis), roll(x, bit, axis))
        bit *= 2
    return x


def exchange_kernel(
    level_in, u_in, v_in, depth_in, tracers_in, land_in,
    level_out, u_out, v_out, tracers_out,
    x, land, packed, packed_t, send_cols, send_rows, got_cols, got_rows, got_corners, halo_t, strip, other,
    load_sem, send_sem, recv_sem,
):
    rows, cols = u_out.shape
    nx, ny = lax.axis_size("gx"), lax.axis_size("gy")
    me_x, me_y = lax.axis_index("gx"), lax.axis_index("gy")
    to_e, to_w = lax.rem(me_x + 1, nx), lax.rem(me_x + nx - 1, nx)
    top, bottom = me_y == ny - 1, me_y == 0
    past = lambda column: jnp.where(top, nx - 1 - column, column)
    to_n, to_s = jnp.where(top, me_y, me_y + 1), jnp.where(bottom, me_y, me_y - 1)
    own_ne, own_nw = top & (past(to_e) == me_x), top & (past(to_w) == me_x)
    has_s = jnp.logical_not(bottom)

    barrier = pltpu.get_barrier_semaphore()

    def greet(to_x, to_y):
        pl.semaphore_signal(barrier, inc=1, device_id=(to_x, to_y), device_id_type=MESH)

    greet(to_w, me_y)
    greet(to_e, me_y)
    greet(past(me_x), to_n)
    pl.when(jnp.logical_not(own_ne))(lambda: greet(past(to_e), to_n))
    pl.when(jnp.logical_not(own_nw))(lambda: greet(past(to_w), to_n))

    @pl.when(has_s)
    def _():
        greet(me_x, to_s)
        greet(to_e, to_s)
        greet(to_w, to_s)

    inner = pl.ds(8, rows)
    loads = [
        pltpu.make_async_copy(land_in, land, load_sem.at[0]),
        pltpu.make_async_copy(u_in, x.at[U, inner], load_sem.at[1]),
        pltpu.make_async_copy(v_in, x.at[V, inner], load_sem.at[2]),
        pltpu.make_async_copy(level_in, x.at[LEVEL, inner], load_sem.at[3]),
        pltpu.make_async_copy(depth_in, x.at[DEPTH, inner], load_sem.at[4]),
        pltpu.make_async_copy(tracers_in, x.at[pl.ds(T0, 2), inner], load_sem.at[5]),
    ]
    for load in loads:
        load.start()
    for f in range(FIELDS):
        x[f, 0:8] = jnp.ones((8, cols), jnp.float32)
        x[f, rows + 8 : rows + 16] = jnp.ones((8, cols), jnp.float32)
    for load in loads:
        load.wait()

    size = 64

    def pack_columns(k, carry):
        at = pl.multiple_of(k * size, size)
        x[MASK, pl.ds(at + 8, size)] = land[pl.ds(at, size)].astype(jnp.float32)
        lane = lanes((size, 128))
        result = None
        for f in range(FIELDS):
            first = x[f, pl.ds(at + 8, size), 0:128]
            last = x[f, pl.ds(at + 8, size), cols - 128 : cols]
            ends = roll(jnp.where(lane < 64, first, last), f * GROUP + 8, 1)
            result = ends if f == 0 else jnp.where(lane < f * GROUP, result, ends)
        packed[pl.ds(at, size)] = result
        return carry

    lax.fori_loop(0, rows // size, pack_columns, 0, unroll=True)
    packed_t[...] = packed[...].T

    def put(ref, at, parts):
        for k, part in enumerate(parts):
            ref[at, 8 * k : 8 * k + 8] = part

    groups = [GROUP * f for f in range(FIELDS)]
    put(send_cols, 0, pack_last([packed_t[g : g + 8] for g in groups]))
    put(send_cols, 1, pack_first([packed_t[g + 8 : g + 16] for g in groups]))
    put(send_rows, 0, pack_last([x[f, rows : rows + 8] for f in range(FIELDS)]))
    put(send_rows, 1, pack_first([x[f, 8:16] for f in range(FIELDS)]))

    def copy(source, target, k, at, to_x, to_y):
        return pltpu.make_async_remote_copy(
            src_ref=source,
            dst_ref=target,
            send_sem=send_sem.at[k],
            recv_sem=recv_sem.at[at],
            device_id=(to_x, to_y),
            device_id_type=MESH,
        )

    north_rows, south_rows = packed.at[pl.ds(rows - 8, 8)], packed.at[pl.ds(0, 8)]
    corner = lambda at: got_corners.at[at - SW]
    away_e = copy(send_cols.at[0], got_cols.at[W], E, W, to_e, me_y)
    away_w = copy(send_cols.at[1], got_cols.at[E], W, E, to_w, me_y)
    away_s = copy(send_rows.at[1], got_rows.at[1], S, N, me_x, to_s)
    away_se = copy(south_rows, corner(NW), SE, NW, to_e, to_s)
    away_sw = copy(south_rows, corner(NE), SW, NE, to_w, to_s)
    away_n = copy(send_rows.at[0], got_rows.at[0], N, S, me_x, to_n)
    away_ne = copy(north_rows, corner(SW), NE, SW, to_e, to_n)
    away_nw = copy(north_rows, corner(SE), NW, SE, to_w, to_n)
    fold_n = copy(send_rows.at[0], got_rows.at[1], N, N, past(me_x), to_n)
    fold_ne = copy(north_rows, corner(NE), NE, NE, past(to_e), to_n)
    fold_nw = copy(north_rows, corner(NW), NW, NW, past(to_w), to_n)
    not_top = jnp.logical_not(top)
    far_ne, far_nw = top & jnp.logical_not(own_ne), top & jnp.logical_not(own_nw)

    count = 3 + jnp.where(own_ne, 0, 1) + jnp.where(own_nw, 0, 1) + jnp.where(has_s, 3, 0)
    pl.semaphore_wait(barrier, count)
    away_e.start()
    away_w.start()

    @pl.when(not_top)
    def _():
        away_ne.start()
        away_nw.start()
        away_n.start()

    @pl.when(top)
    def _():
        fold_n.start()

    pl.when(far_ne)(lambda: fold_ne.start())
    pl.when(far_nw)(lambda: fold_nw.start())

    @pl.when(has_s)
    def _():
        away_se.start()
        away_sw.start()
        away_s.start()

    def coriolis(row):
        row = row.astype(jnp.float32)
        total = 1.0 * ny * rows
        return CORIOLIS_TOP * ((row + 0.5) / total), CORIOLIS_TOP * ((row + 1.0) / total)

    def compute_inner(k, carry):
        at = pl.multiple_of(k * BLOCK, BLOCK)
        part = [x[f, pl.ds(at, BLOCK + 16)] for f in range(FIELDS)]
        row = me_y * rows + at - 8 + sublanes((BLOCK + 16, 1))
        out = advance(*part[:5], part[5:], *coriolis(row), 0)
        keep = pl.ds(at, BLOCK)
        level_out[keep] = out[0][8 : BLOCK + 8]
        u_out[keep] = out[1][8 : BLOCK + 8]
        v_out[keep] = out[2][8 : BLOCK + 8]
        tracers_out[0, keep] = out[3][8 : BLOCK + 8]
        tracers_out[1, keep] = out[4][8 : BLOCK + 8]
        return carry

    lax.fori_loop(0, rows // BLOCK, compute_inner, 0)

    away_w.wait_recv()
    away_e.wait_recv()
    away_s.wait_recv()

    @pl.when(has_s)
    def _():
        away_n.wait_recv()
        away_ne.wait_recv()
        away_nw.wait_recv()

    pl.when(jnp.logical_not(own_nw))(lambda: away_se.wait_recv())
    pl.when(jnp.logical_not(own_ne))(lambda: away_sw.wait_recv())

    @pl.when(own_nw)
    def _():
        corner(NW)[...] = north_rows[...]

    @pl.when(own_ne)
    def _():
        corner(NE)[...] = north_rows[...]

    from_w, from_e = unpack_last(got_cols.at[W]), unpack_first(got_cols.at[E])
    for f, g in enumerate(groups):
        halo_t[g : g + 8] = from_w[f]
        halo_t[g + 8 : g + 16] = from_e[f]
    halo_t[GROUP * FIELDS :] = jnp.ones((128 - GROUP * FIELDS, rows), jnp.float32)

    def put_rows(at, parts, sides):
        for f in range(FIELDS):
            strip[f, at : at + 8, 0:cols] = parts[f]
            strip[f, at : at + 8, cols : cols + 128] = roll(sides, -(GROUP * f + 8), 1)

    put_rows(0, [x[f, rows : rows + 8] for f in range(FIELDS)], halo_t[:, rows - 128 : rows].T[120:128])
    put_rows(24, [x[f, 8:16] for f in range(FIELDS)], halo_t[:, 0:128].T[0:8])
    eastern = lanes((8, 128)) & 8 != 0

    @pl.when(not_top)
    def _():
        put_rows(8, unpack_first(got_rows.at[1]), jnp.where(eastern, corner(NE)[...], corner(NW)[...]))
        other[...] = jnp.zeros_like(other)

    @pl.when(top)
    def _():
        parts = [flip(part, 0, 8) for part in unpack_last(got_rows.at[1])]
        tiles = range(0, cols, 128)
        parts = [
            jnp.concatenate([flip(part[:, c : c + 128], 1, 128) for c in reversed(tiles)], axis=1)
            for part in parts
        ]
        sides = jnp.where(eastern, corner(NW)[...], corner(NE)[...])
        put_rows(8, parts, flip(flip(sides, 0, 8), 1, GROUP))
        strip[U, 8:16] = -roll(strip[U, 8:16], -1, 1)
        mirrored = strip[V, 8:16]
        strip[V, 8:16] = -roll(mirrored, -1, 0)
        other[...] = roll(mirrored, -1, 0)

    @pl.when(has_s)
    def _():
        put_rows(16, unpack_last(got_rows.at[0]), jnp.where(eastern, corner(SE)[...], corner(SW)[...]))

    @pl.when(bottom)
    def _():
        for f in range(FIELDS):
            strip[f, 16:24] = jnp.full((8, cols + 128), 1.0 if f == DEPTH else 0.0, jnp.float32)

    parts = [
        jnp.concatenate([packed_t[g : g + 8], halo_t[g + 8 : g + 16], halo_t[g : g + 8], packed_t[g + 8 : g + 16]], axis=0)
        for g in groups
    ]
    row = me_y * rows + lanes((1, rows))
    by_col = advance(*parts[:5], parts[5:], *coriolis(row), 1)

    s = sublanes((32, 1))
    row = me_y * rows + jnp.where(s < 16, rows - 8 + s, s - 24)
    total = ny * rows
    cor_u = coriolis(jnp.where(row >= total, 2 * total - 1 - row, row))[0]
    cor_v = coriolis(jnp.where(row >= total, 2 * total - 2 - row, row))[1]
    parts = [strip[f] for f in range(FIELDS)]
    at_fold = top & (sublanes((8, cols + 128)) == 7)
    by_row = advance(*parts[:5], parts[5:], cor_u, cor_v, 0, (at_fold, other[...]))

    zeros = jnp.zeros((128 - GROUP * 5, rows), jnp.float32)
    back = jnp.concatenate([part for o in by_col for part in (o[0:8], o[24:32])] + [zeros], axis=0).T
    outs = [level_out, u_out, v_out, tracers_out.at[0], tracers_out.at[1]]
    lane = lanes((rows, 128))
    s = sublanes((8, cols))
    for o, out in enumerate(outs):
        ends = roll(back, -(GROUP * o + 8), 1)
        out[:, 0:128] = jnp.where(lane < 4, ends, out[:, 0:128])
        out[:, cols - 128 : cols] = jnp.where(lane >= 124, ends, out[:, cols - 128 : cols])
        out[0:8] = jnp.where(s < 4, by_row[o][24:32, 0:cols], out[0:8])
        out[rows - 8 : rows] = jnp.where(s >= 4, by_row[o][0:8, 0:cols], out[rows - 8 : rows])

    away_e.wait_send()
    away_w.wait_send()

    @pl.when(not_top)
    def _():
        away_ne.wait_send()
        away_nw.wait_send()
        away_n.wait_send()

    @pl.when(top)
    def _():
        fold_n.wait_send()

    pl.when(far_ne)(lambda: fold_ne.wait_send())
    pl.when(far_nw)(lambda: fold_nw.wait_send())

    @pl.when(has_s)
    def _():
        away_se.wait_send()
        away_sw.wait_send()
        away_s.wait_send()


def store_kernel(count, *refs):
    sems = refs[-1]
    copies = [pltpu.make_async_copy(refs[k], refs[count + k], sems.at[k]) for k in range(count)]
    for one in copies:
        one.start()
    for one in copies:
        one.wait()


def local(sea_level, transport_u, transport_v, ocean_depth, tracers, land_mask):
    rows, cols = sea_level.shape
    f32 = jnp.float32
    plane, pair = jax.ShapeDtypeStruct((rows, cols), f32), jax.ShapeDtypeStruct((2, rows, cols), f32)
    shapes = [plane, plane, plane, pair]
    anywhere, vmem = pl.BlockSpec(memory_space=pl.ANY), pl.BlockSpec(memory_space=pltpu.VMEM)
    held = pl.pallas_call(
        exchange_kernel,
        out_shape=[MEM(s.shape, s.dtype) for s in shapes],
        in_specs=[anywhere] * 6,
        out_specs=[vmem] * 4,
        scratch_shapes=[
            pltpu.VMEM((FIELDS, rows + 16, cols), f32),
            pltpu.VMEM((rows, cols), jnp.int32),
            pltpu.VMEM((rows, 128), f32),
            pltpu.VMEM((128, rows), f32),
            pltpu.VMEM((2, 24, rows), f32),
            pltpu.VMEM((2, 24, cols), f32),
            pltpu.VMEM((2, 24, rows), f32),
            pltpu.VMEM((2, 24, cols), f32),
            pltpu.VMEM((4, 8, 128), f32),
            pltpu.VMEM((128, rows), f32),
            pltpu.VMEM((FIELDS, 32, cols + 128), f32),
            pltpu.VMEM((8, cols + 128), f32),
            pltpu.SemaphoreType.DMA((6,)),
            pltpu.SemaphoreType.DMA((8,)),
            pltpu.SemaphoreType.DMA((8,)),
        ],
        compiler_params=pltpu.CompilerParams(collective_id=0, has_side_effects=True, vmem_limit_bytes=32 * 2**20),
        name="exchange",
    )(sea_level, transport_u, transport_v, ocean_depth, tracers, land_mask)
    return pl.pallas_call(
        functools.partial(store_kernel, len(shapes)),
        out_shape=shapes,
        in_specs=[IN] * 4,
        out_specs=[anywhere] * 4,
        scratch_shapes=[pltpu.SemaphoreType.DMA((len(shapes),))],
        name="store",
    )(*held)


MEM = pltpu.VMEM
IN = pl.BlockSpec(memory_space=pltpu.VMEM)


def solution(mesh):
    spread, tracers = P("gy", "gx"), P(None, "gy", "gx")
    return jax.shard_map(
        local,
        mesh=mesh,
        in_specs=(spread, spread, spread, spread, tracers, spread),
        out_specs=(spread, spread, spread, tracers),
        check_vma=False,
    )
```

time: 543 us -> 42.8 us (0.08); the launches traced: 533 us -> 42.4 us
  starting transfers between devices: 301 us -> 0 us
  waiting for transfers between devices: 177 us -> 0 us
  Pallas kernels: 0 us -> 32.5 us
  other arithmetic: 23 us -> 0 us
  local copies, waits for them, and re-layouts: 29.8 us -> 9.25 us
    ppermute x64 -> x0, starting transfers between devices: 301 us -> none  [the longest x40 147 us: swapped(): return lax.ppermute(value, axis, pairs)]
    ppermute x64 -> x0, waiting for transfers between devices: 177 us -> none  [the longest x40 100 us: swapped(): return lax.ppermute(value, axis, pairs)]
    pallas_call x0 -> x2, Pallas kernels: none -> 32.5 us  [the longest x1 29.7 us: local(): pl.pallas_call(exchange_kernel, out_shape=[MEM(s.shape, s.dtype) for s in...]
    slice x52 -> x0, local copies, waits for them, and re-layouts: 18.8 us -> none  [the longest x6 3.61 us: take_north(): return shifted(field[..., :1, :], 'gy', -1)]
    mul x8 -> x0, other arithmetic: 8.38 us -> none  [the longest x2 3.72 us: local(): north_mask * ((1.0 - DRAG_RATE / depth_v) * north_sym - GRAVITY_STEP * de...]
  transfers between devices with their start and end apart: 64 -> 0, of which waited for: 41 -> 0; matrix products, arithmetic and copies ran while one was open for 6% -> 0% of each run, Pallas kernels for 0% -> 0%
where the time goes in v1:
time: 42.8 us; the launch traced here: 42.4 us
  Pallas kernels  32.5 us (76%)
  local copies, waits for them, and re-layouts  9.25 us (22%)
  between operations  0.67 us (2%)
    pallas_call x1, Pallas kernels, local(): pl.pallas_call(exchange_kernel, out_shape=[MEM(s.shape, s.dtype) for s in...  29.7 us
    unnamed x20, local copies, waits for them, and re-layouts  9.25 us
    pallas_call x1, Pallas kernels, local(): pl.pallas_call(functools.partial(store_kernel, len(shapes)), out_shape=sh...  2.79 us

profile of v1, /device:TPU:1, one launch (start us, length us, event | category | flops | bytes accessed | tf_op | source)
XLA Modules:
  0.0 42.4 jit_solution(7697025579498905392)
XLA Ops:
  0.6 0.0 copy-start
  0.6 1.1 %copy-done = f32[2,256,384]{2,1,0:T(8,128)S(1)} copy-done((f32[2,256,384]{2,1,0:T(8,128)S(1)}, f32[2,256,384]{2,1,0:T(8,128)}, u32[]{:S(2)}) %copy-start) | copy-done | bytes 786456
  1.8 0.0 copy-start.2
  1.8 1.0 %copy-done.2 = f32[256,384]{1,0:T(8,128)S(1)} copy-done((f32[256,384]{1,0:T(8,128)S(1)}, f32[256,384]{1,0:T(8,128)}, u32[]{:S(2)}) %copy-start.2) | copy-done | bytes 393240
  2.8 0.0 copy-start.3
  2.8 1.0 %copy-done.3 = f32[256,384]{1,0:T(8,128)S(1)} copy-done((f32[256,384]{1,0:T(8,128)S(1)}, f32[256,384]{1,0:T(8,128)}, u32[]{:S(2)}) %copy-start.3) | copy-done | bytes 393240
  3.8 0.0 copy-start.4
  3.8 1.0 %copy-done.4 = f32[256,384]{1,0:T(8,128)S(1)} copy-done((f32[256,384]{1,0:T(8,128)S(1)}, f32[256,384]{1,0:T(8,128)}, u32[]{:S(2)}) %copy-start.4) | copy-done | bytes 393240
  4.8 0.0 copy-start.5
  4.8 1.0 %copy-done.5 = f32[256,384]{1,0:T(8,128)S(1)} copy-done((f32[256,384]{1,0:T(8,128)S(1)}, f32[256,384]{1,0:T(8,128)}, u32[]{:S(2)}) %copy-start.5) | copy-done | bytes 393240
  5.8 0.0 copy-start.6
  5.8 1.0 %copy-done.6 = s32[256,384]{1,0:T(8,128)S(1)} copy-done((s32[256,384]{1,0:T(8,128)S(1)}, s32[256,384]{1,0:T(8,128)}, u32[]{:S(2)}) %copy-start.6) | copy-done | bytes 393240
  6.7 29.7 %exchange.1 = (f32[256,384]{1,0:T(8,128)S(1)}, f32[256,384]{1,0:T(8,128)S(1)}, f32[256,384]{1,0:T(8,128)S(1)}, f32[2,256,384]{2,1,0:T(8,128)S(1)}) custom-call(f32[256,384]{1,0:T(8,128)S(1)} %copy-done.2, f32[256,384]{1,0:T(8,128)S(1)} %copy-done.3, f32[256,384]{1,0:T(8,128)S(1)} %copy-done.4, f32[256,384]{1,0:T(8,128)S(1)} %copy-done.5, ...), custom_call_target="tpu_custom_call" | custom-call | tf_op jit(solution)/shard_map/exchange/pallas_call | solution.py:413
  36.5 0.0 copy-start.1
  36.5 0.9 %copy-done.1 = f32[2,256,384]{2,1,0:T(8,128)} copy-done((f32[2,256,384]{2,1,0:T(8,128)}, f32[2,256,384]{2,1,0:T(8,128)S(1)}, u32[]{:S(2)}) %copy-start.1) | copy-done | bytes 786456
  37.3 0.0 copy-start.7
  37.3 0.8 %copy-done.7 = f32[256,384]{1,0:T(8,128)} copy-done((f32[256,384]{1,0:T(8,128)}, f32[256,384]{1,0:T(8,128)S(1)}, u32[]{:S(2)}) %copy-start.7) | copy-done | bytes 393240
  38.1 0.0 copy-start.8
  38.1 0.8 %copy-done.8 = f32[256,384]{1,0:T(8,128)} copy-done((f32[256,384]{1,0:T(8,128)}, f32[256,384]{1,0:T(8,128)S(1)}, u32[]{:S(2)}) %copy-start.8) | copy-done | bytes 393240
  38.9 0.0 copy-start.9
  38.9 0.7 %copy-done.9 = f32[256,384]{1,0:T(8,128)} copy-done((f32[256,384]{1,0:T(8,128)}, f32[256,384]{1,0:T(8,128)S(1)}, u32[]{:S(2)}) %copy-start.9) | copy-done | bytes 393240
  39.6 2.8 %store.1 = (f32[256,384]{1,0:T(8,128)}, f32[256,384]{1,0:T(8,128)}, f32[256,384]{1,0:T(8,128)}, f32[2,256,384]{2,1,0:T(8,128)}) custom-call(f32[256,384]{1,0:T(8,128)} %copy-done.7, f32[256,384]{1,0:T(8,128)} %copy-done.8, f32[256,384]{1,0:T(8,128)} %copy-done.9, f32[2,256,384]{2,1,0:T(8,128)} %copy-done.1), custom_call_target="tpu_custom_call" | custom-call | tf_op jit(solution)/shard_map/store/pallas_call | solution.py:438
Async XLA Ops:
  0.6 1.1 %copy-start = (f32[2,256,384]{2,1,0:T(8,128)S(1)}, f32[2,256,384]{2,1,0:T(8,128)}, u32[]{:S(2)}) copy-start(f32[2,256,384]{2,1,0:T(8,128)} %tracers_in.1) | copy-start | bytes 2359300
  1.8 1.0 %copy-start.2 = (f32[256,384]{1,0:T(8,128)S(1)}, f32[256,384]{1,0:T(8,128)}, u32[]{:S(2)}) copy-start(f32[256,384]{1,0:T(8,128)} %level_in.1) | copy-start | bytes 1179652
  2.8 1.0 %copy-start.3 = (f32[256,384]{1,0:T(8,128)S(1)}, f32[256,384]{1,0:T(8,128)}, u32[]{:S(2)}) copy-start(f32[256,384]{1,0:T(8,128)} %u_in.1) | copy-start | bytes 1179652
  3.8 1.0 %copy-start.4 = (f32[256,384]{1,0:T(8,128)S(1)}, f32[256,384]{1,0:T(8,128)}, u32[]{:S(2)}) copy-start(f32[256,384]{1,0:T(8,128)} %v_in.1) | copy-start | bytes 1179652
  4.8 1.0 %copy-start.5 = (f32[256,384]{1,0:T(8,128)S(1)}, f32[256,384]{1,0:T(8,128)}, u32[]{:S(2)}) copy-start(f32[256,384]{1,0:T(8,128)} %depth_in.1) | copy-start | bytes 1179652
  5.8 1.0 %copy-start.6 = (s32[256,384]{1,0:T(8,128)S(1)}, s32[256,384]{1,0:T(8,128)}, u32[]{:S(2)}) copy-start(s32[256,384]{1,0:T(8,128)} %land_in.1) | copy-start | bytes 1179652
  36.5 0.9 %copy-start.1 = (f32[2,256,384]{2,1,0:T(8,128)}, f32[2,256,384]{2,1,0:T(8,128)S(1)}, u32[]{:S(2)}) copy-start(f32[2,256,384]{2,1,0:T(8,128)S(1)} %get-tuple-element.11.refs_3_) | copy-start | bytes 2359300
  37.3 0.8 %copy-start.7 = (f32[256,384]{1,0:T(8,128)}, f32[256,384]{1,0:T(8,128)S(1)}, u32[]{:S(2)}) copy-start(f32[256,384]{1,0:T(8,128)S(1)} %get-tuple-element.8.refs_0_) | copy-start | bytes 1179652
  38.1 0.8 %copy-start.8 = (f32[256,384]{1,0:T(8,128)}, f32[256,384]{1,0:T(8,128)S(1)}, u32[]{:S(2)}) copy-start(f32[256,384]{1,0:T(8,128)S(1)} %get-tuple-element.9.refs_1_) | copy-start | bytes 1179652
  38.9 0.7 %copy-start.9 = (f32[256,384]{1,0:T(8,128)}, f32[256,384]{1,0:T(8,128)S(1)}, u32[]{:S(2)}) copy-start(f32[256,384]{1,0:T(8,128)S(1)} %get-tuple-element.10.refs_2_) | copy-start | bytes 1179652

commit v2 on v1

--- a/solution.py
+++ b/solution.py
@@ -94,32 +94,67 @@
     return level, u, v, new[0], new[1]
 
 
-def pack_last(x):
+def pack_last(narrow, wide, x):
     s = sublanes(x[0].shape)
     return [
-        jnp.where(s < 4, roll(x[U], 4, 0), x[V]),
-        jnp.where(s < 4, roll(x[LEVEL], 4, 0), x[MASK]),
-        jnp.where(s < 4, roll(x[DEPTH], 4, 0), jnp.where(s < 6, roll(x[T0], 6, 0), x[T1])),
+        jnp.where(s < 1, roll(x[T0], 1, 0), jnp.where(s < 4, roll(x[narrow], 4, 0), x[wide])),
+        jnp.where(s < 1, roll(x[T1], 1, 0), jnp.where(s < 4, roll(x[LEVEL], 4, 0), x[MASK])),
+        x[DEPTH],
     ]
 
 
-def pack_first(x):
+def pack_first(narrow, wide, x):
     s = sublanes(x[0].shape)
     return [
-        jnp.where(s < 4, x[U], roll(x[V], 4, 0)),
-        jnp.where(s < 4, x[LEVEL], roll(x[MASK], 4, 0)),
-        jnp.where(s < 4, x[DEPTH], jnp.where(s < 6, roll(x[T0], 4, 0), roll(x[T1], 6, 0))),
+        jnp.where(s < 3, x[narrow], jnp.where(s < 4, roll(x[T0], 3, 0), roll(x[wide], 4, 0))),
+        jnp.where(s < 3, x[LEVEL], jnp.where(s < 4, roll(x[T1], 3, 0), roll(x[MASK], 4, 0))),
+        x[DEPTH],
     ]
 
 
-def unpack_last(ref):
-    a, b, c = ref[0:8], ref[8:16], ref[16:24]
-    return [roll(a, 4, 0), a, roll(b, 4, 0), b, roll(c, 4, 0), roll(c, 2, 0), c]
-
-
-def unpack_first(ref):
-    a, b, c = ref[0:8], ref[8:16], ref[16:24]
-    return [a, roll(a, 4, 0), b, roll(b, 4, 0), c, roll(c, 4, 0), roll(c, 2, 0)]
+def unpack_last(narrow, wide, a, b, c):
+    x = {narrow: roll(a, 4, 0), wide: a, LEVEL: roll(b, 4, 0), MASK: b, DEPTH: c, T0: roll(a, 7, 0), T1: roll(b, 7, 0)}
+    return [x[f] for f in range(FIELDS)]
+
+
+def unpack_first(narrow, wide, a, b, c):
+    x = {narrow: a, wide: roll(a, 4, 0), LEVEL: b, MASK: roll(b, 4, 0), DEPTH: c, T0: roll(a, 5, 0), T1: roll(b, 5, 0)}
+    return [x[f] for f in range(FIELDS)]
+
+
+def put_columns(ref, parts, last):
+    a, b, c = parts
+    half = c.shape[1] // 2
+    left, right = c[:, :half], c[:, half:]
+    upper = sublanes(left.shape) < 4
+    both = jnp.where(upper, roll(left, 4, 0), right) if last else jnp.where(upper, left, roll(right, 4, 0))
+    for k, part in enumerate([a[:, :half], a[:, half:], b[:, :half], b[:, half:], both]):
+        ref[8 * k : 8 * k + 8] = part
+
+
+def get_columns(ref, last):
+    both = ref[32:40]
+    left, right = (roll(both, 4, 0), both) if last else (both, roll(both, 4, 0))
+    pairs = [(ref[0:8], ref[8:16]), (ref[16:24], ref[24:32]), (left, right)]
+    return [jnp.concatenate(pair, axis=1) for pair in pairs]
+
+
+def pack_corner(x, first_row, first_lane):
+    row, lane = sublanes(x.shape), lanes(x.shape)
+    total = jnp.zeros_like(x)
+    for r in range(4):
+        here = (row == first_row + r) & (lane & 12 == 4 * r)
+        total = total + jnp.where(here, roll(x, 4 * r - first_lane, 1), 0.0)
+    return jnp.sum(total, axis=0, keepdims=True)
+
+
+def unpack_corner(x, first_row, first_lane, base):
+    x = jnp.broadcast_to(x, (8, 128))
+    row, lane = sublanes(x.shape), lanes(x.shape)
+    for r in range(4):
+        here = (row == first_row + r) & (lane & 12 == first_lane)
+        base = jnp.where(here, roll(x, first_lane - 4 * r, 1), base)
+    return base
 
 
 def flip(x, axis, group):
@@ -134,7 +169,7 @@
 def exchange_kernel(
     level_in, u_in, v_in, depth_in, tracers_in, land_in,
     level_out, u_out, v_out, tracers_out,
-    x, land, packed, packed_t, send_cols, send_rows, got_cols, got_rows, got_corners, halo_t, strip, other,
+    x, land, packed, packed_t, send_cols, send_rows, send_corners, got_cols, got_rows, got_corners, halo_t, strip, other,
     load_sem, send_sem, recv_sem,
 ):
     rows, cols = u_out.shape
@@ -199,65 +234,16 @@
     lax.fori_loop(0, rows // size, pack_columns, 0, unroll=True)
     packed_t[...] = packed[...].T
 
-    def put(ref, at, parts):
-        for k, part in enumerate(parts):
-            ref[at, 8 * k : 8 * k + 8] = part
-
     groups = [GROUP * f for f in range(FIELDS)]
-    put(send_cols, 0, pack_last([packed_t[g : g + 8] for g in groups]))
-    put(send_cols, 1, pack_first([packed_t[g + 8 : g + 16] for g in groups]))
-    put(send_rows, 0, pack_last([x[f, rows : rows + 8] for f in range(FIELDS)]))
-    put(send_rows, 1, pack_first([x[f, 8:16] for f in range(FIELDS)]))
-
-    def copy(source, target, k, at, to_x, to_y):
-        return pltpu.make_async_remote_copy(
-            src_ref=source,
-            dst_ref=target,
-            send_sem=send_sem.at[k],
-            recv_sem=recv_sem.at[at],
-            device_id=(to_x, to_y),
-            device_id_type=MESH,
-        )
-
-    north_rows, south_rows = packed.at[pl.ds(rows - 8, 8)], packed.at[pl.ds(0, 8)]
-    corner = lambda at: got_corners.at[at - SW]
-    away_e = copy(send_cols.at[0], got_cols.at[W], E, W, to_e, me_y)
-    away_w = copy(send_cols.at[1], got_cols.at[E], W, E, to_w, me_y)
-    away_s = copy(send_rows.at[1], got_rows.at[1], S, N, me_x, to_s)
-    away_se = copy(south_rows, corner(NW), SE, NW, to_e, to_s)
-    away_sw = copy(south_rows, corner(NE), SW, NE, to_w, to_s)
-    away_n = copy(send_rows.at[0], got_rows.at[0], N, S, me_x, to_n)
-    away_ne = copy(north_rows, corner(SW), NE, SW, to_e, to_n)
-    away_nw = copy(north_rows, corner(SE), NW, SE, to_w, to_n)
-    fold_n = copy(send_rows.at[0], got_rows.at[1], N, N, past(me_x), to_n)
-    fold_ne = copy(north_rows, corner(NE), NE, NE, past(to_e), to_n)
-    fold_nw = copy(north_rows, corner(NW), NW, NW, past(to_w), to_n)
-    not_top = jnp.logical_not(top)
-    far_ne, far_nw = top & jnp.logical_not(own_ne), top & jnp.logical_not(own_nw)
-
-    count = 3 + jnp.where(own_ne, 0, 1) + jnp.where(own_nw, 0, 1) + jnp.where(has_s, 3, 0)
-    pl.semaphore_wait(barrier, count)
-    away_e.start()
-    away_w.start()
-
-    @pl.when(not_top)
-    def _():
-        away_ne.start()
-        away_nw.start()
-        away_n.start()
-
-    @pl.when(top)
-    def _():
-        fold_n.start()
-
-    pl.when(far_ne)(lambda: fold_ne.start())
-    pl.when(far_nw)(lambda: fold_nw.start())
-
-    @pl.when(has_s)
-    def _():
-        away_se.start()
-        away_sw.start()
-        away_s.start()
+    north_end, south_end = packed[rows - 8 : rows], packed[0:8]
+    send_corners[NE - SW] = pack_corner(north_end, 4, 4)
+    send_corners[NW - SW] = pack_corner(north_end, 4, 8)
+    send_corners[SE - SW] = pack_corner(south_end, 0, 4)
+    send_corners[SW - SW] = pack_corner(south_end, 0, 8)
+    put_columns(send_cols.at[0], pack_last(V, U, [packed_t[g : g + 8] for g in groups]), True)
+    put_columns(send_cols.at[1], pack_first(V, U, [packed_t[g + 8 : g + 16] for g in groups]), False)
+    send_rows[0] = jnp.concatenate(pack_last(U, V, [x[f, rows : rows + 8] for f in range(FIELDS)]), axis=0)
+    send_rows[1] = jnp.concatenate(pack_first(U, V, [x[f, 8:16] for f in range(FIELDS)]), axis=0)
 
     def coriolis(row):
         row = row.astype(jnp.float32)
@@ -277,7 +263,57 @@
         tracers_out[1, keep] = out[4][8 : BLOCK + 8]
         return carry
 
-    lax.fori_loop(0, rows // BLOCK, compute_inner, 0)
+    blocks = rows // BLOCK
+    sends_first = lax.rem(me_x, 2)
+    lax.fori_loop(0, blocks * (1 - sends_first), compute_inner, 0)
+
+    def copy(source, target, k, at, to_x, to_y):
+        return pltpu.make_async_remote_copy(
+            src_ref=source,
+            dst_ref=target,
+            send_sem=send_sem.at[k],
+            recv_sem=recv_sem.at[at],
+            device_id=(to_x, to_y),
+            device_id_type=MESH,
+        )
+
+    def corner(k, at, to_x, to_y):
+        return copy(send_corners.at[k - SW], got_corners.at[at - SW], k, at, to_x, to_y)
+
+    away_e = copy(send_cols.at[0], got_cols.at[0], E, W, to_e, me_y)
+    away_w = copy(send_cols.at[1], got_cols.at[1], W, E, to_w, me_y)
+    away_s = copy(send_rows.at[1], got_rows.at[1], S, N, me_x, to_s)
+    away_n = copy(send_rows.at[0], got_rows.at[0], N, S, me_x, to_n)
+    fold_n = copy(send_rows.at[0], got_rows.at[1], N, N, past(me_x), to_n)
+    away_se, away_sw = corner(SE, NW, to_e, to_s), corner(SW, NE, to_w, to_s)
+    away_ne, away_nw = corner(NE, SW, to_e, to_n), corner(NW, SE, to_w, to_n)
+    fold_ne, fold_nw = corner(NE, NE, past(to_e), to_n), corner(NW, NW, past(to_w), to_n)
+    not_top = jnp.logical_not(top)
+    far_ne, far_nw = top & jnp.logical_not(own_ne), top & jnp.logical_not(own_nw)
+
+    count = 3 + jnp.where(own_ne, 0, 1) + jnp.where(own_nw, 0, 1) + jnp.where(has_s, 3, 0)
+    pl.semaphore_wait(barrier, count)
+
+    @pl.when(not_top)
+    def _():
+        away_n.start()
+        away_ne.start()
+        away_nw.start()
+
+    pl.when(top)(lambda: fold_n.start())
+    pl.when(far_ne)(lambda: fold_ne.start())
+    pl.when(far_nw)(lambda: fold_nw.start())
+
+    @pl.when(has_s)
+    def _():
+        away_s.start()
+        away_se.start()
+        away_sw.start()
+
+    away_e.start()
+    away_w.start()
+
+    lax.fori_loop(blocks * (1 - sends_first), blocks, compute_inner, 0)
 
     away_w.wait_recv()
     away_e.wait_recv()
@@ -294,13 +330,14 @@
 
     @pl.when(own_nw)
     def _():
-        corner(NW)[...] = north_rows[...]
+        got_corners[NW - SW] = send_corners[NW - SW]
 
     @pl.when(own_ne)
     def _():
-        corner(NE)[...] = north_rows[...]
-
-    from_w, from_e = unpack_last(got_cols.at[W]), unpack_first(got_cols.at[E])
+        got_corners[NE - SW] = send_corners[NE - SW]
+
+    from_w = unpack_last(V, U, *get_columns(got_cols.at[0], True))
+    from_e = unpack_first(V, U, *get_columns(got_cols.at[1], False))
     for f, g in enumerate(groups):
         halo_t[g : g + 8] = from_w[f]
         halo_t[g + 8 : g + 16] = from_e[f]
@@ -313,23 +350,26 @@
 
     put_rows(0, [x[f, rows : rows + 8] for f in range(FIELDS)], halo_t[:, rows - 128 : rows].T[120:128])
     put_rows(24, [x[f, 8:16] for f in range(FIELDS)], halo_t[:, 0:128].T[0:8])
-    eastern = lanes((8, 128)) & 8 != 0
+    from_n, from_s = ([ref[0:8], ref[8:16], ref[16:24]] for ref in (got_rows.at[1], got_rows.at[0]))
+    from_ne, from_nw, from_se, from_sw = (got_corners[k - SW] for k in (NE, NW, SE, SW))
+    nothing = jnp.zeros((8, 128), jnp.float32)
 
     @pl.when(not_top)
     def _():
-        put_rows(8, unpack_first(got_rows.at[1]), jnp.where(eastern, corner(NE)[...], corner(NW)[...]))
+        sides = unpack_corner(from_ne, 0, 8, unpack_corner(from_nw, 0, 4, nothing))
+        put_rows(8, unpack_first(U, V, *from_n), sides)
         other[...] = jnp.zeros_like(other)
 
     @pl.when(top)
     def _():
-        parts = [flip(part, 0, 8) for part in unpack_last(got_rows.at[1])]
+        parts = [flip(part, 0, 8) for part in unpack_last(U, V, *from_n)]
         tiles = range(0, cols, 128)
         parts = [
             jnp.concatenate([flip(part[:, c : c + 128], 1, 128) for c in reversed(tiles)], axis=1)
             for part in parts
         ]
-        sides = jnp.where(eastern, corner(NW)[...], corner(NE)[...])
-        put_rows(8, parts, flip(flip(sides, 0, 8), 1, GROUP))
+        sides = unpack_corner(flip(from_nw, 1, GROUP), 0, 4, nothing)
+        put_rows(8, parts, unpack_corner(flip(from_ne, 1, GROUP), 0, 8, sides))
         strip[U, 8:16] = -roll(strip[U, 8:16], -1, 1)
         mirrored = strip[V, 8:16]
         strip[V, 8:16] = -roll(mirrored, -1, 0)
@@ -337,31 +377,40 @@
 
     @pl.when(has_s)
     def _():
-        put_rows(16, unpack_last(got_rows.at[0]), jnp.where(eastern, corner(SE)[...], corner(SW)[...]))
+        sides = unpack_corner(from_se, 4, 8, unpack_corner(from_sw, 4, 4, nothing))
+        put_rows(16, unpack_last(U, V, *from_s), sides)
 
     @pl.when(bottom)
     def _():
         for f in range(FIELDS):
             strip[f, 16:24] = jnp.full((8, cols + 128), 1.0 if f == DEPTH else 0.0, jnp.float32)
 
+    upper = sublanes((8, rows)) < 4
     parts = [
-        jnp.concatenate([packed_t[g : g + 8], halo_t[g + 8 : g + 16], halo_t[g : g + 8], packed_t[g + 8 : g + 16]], axis=0)
+        jnp.concatenate(
+            [packed_t[g : g + 8], jnp.where(upper, halo_t[g + 8 : g + 16], halo_t[g : g + 8]), packed_t[g + 8 : g + 16]],
+            axis=0,
+        )
         for g in groups
     ]
     row = me_y * rows + lanes((1, rows))
     by_col = advance(*parts[:5], parts[5:], *coriolis(row), 1)
 
-    s = sublanes((32, 1))
-    row = me_y * rows + jnp.where(s < 16, rows - 8 + s, s - 24)
+    s = sublanes((24, 1))
+    row = me_y * rows + jnp.where(s < 12, rows - 8 + s, s - 16)
     total = ny * rows
     cor_u = coriolis(jnp.where(row >= total, 2 * total - 1 - row, row))[0]
     cor_v = coriolis(jnp.where(row >= total, 2 * total - 2 - row, row))[1]
-    parts = [strip[f] for f in range(FIELDS)]
+    upper = sublanes((8, cols + 128)) < 4
+    parts = [
+        jnp.concatenate([strip[f, 0:8], jnp.where(upper, strip[f, 8:16], strip[f, 16:24]), strip[f, 24:32]], axis=0)
+        for f in range(FIELDS)
+    ]
     at_fold = top & (sublanes((8, cols + 128)) == 7)
     by_row = advance(*parts[:5], parts[5:], cor_u, cor_v, 0, (at_fold, other[...]))
 
     zeros = jnp.zeros((128 - GROUP * 5, rows), jnp.float32)
-    back = jnp.concatenate([part for o in by_col for part in (o[0:8], o[24:32])] + [zeros], axis=0).T
+    back = jnp.concatenate([part for o in by_col for part in (o[0:8], o[16:24])] + [zeros], axis=0).T
     outs = [level_out, u_out, v_out, tracers_out.at[0], tracers_out.at[1]]
     lane = lanes((rows, 128))
     s = sublanes((8, cols))
@@ -369,7 +418,7 @@
         ends = roll(back, -(GROUP * o + 8), 1)
         out[:, 0:128] = jnp.where(lane < 4, ends, out[:, 0:128])
         out[:, cols - 128 : cols] = jnp.where(lane >= 124, ends, out[:, cols - 128 : cols])
-        out[0:8] = jnp.where(s < 4, by_row[o][24:32, 0:cols], out[0:8])
+        out[0:8] = jnp.where(s < 4, by_row[o][16:24, 0:cols], out[0:8])
         out[rows - 8 : rows] = jnp.where(s >= 4, by_row[o][0:8, 0:cols], out[rows - 8 : rows])
 
     away_e.wait_send()
@@ -404,8 +453,8 @@
         one.wait()
 
 
-def local(sea_level, transport_u, transport_v, ocean_depth, tracers, land_mask):
-    rows, cols = sea_level.shape
+def local(*arguments):
+    rows, cols = arguments[0].shape
     f32 = jnp.float32
     plane, pair = jax.ShapeDtypeStruct((rows, cols), f32), jax.ShapeDtypeStruct((2, rows, cols), f32)
     shapes = [plane, plane, plane, pair]
@@ -420,11 +469,12 @@
             pltpu.VMEM((rows, cols), jnp.int32),
             pltpu.VMEM((rows, 128), f32),
             pltpu.VMEM((128, rows), f32),
-            pltpu.VMEM((2, 24, rows), f32),
+            pltpu.VMEM((2, 40, rows // 2), f32),
             pltpu.VMEM((2, 24, cols), f32),
-            pltpu.VMEM((2, 24, rows), f32),
+            pltpu.VMEM((4, 1, 128), f32),
+            pltpu.VMEM((2, 40, rows // 2), f32),
             pltpu.VMEM((2, 24, cols), f32),
-            pltpu.VMEM((4, 8, 128), f32),
+            pltpu.VMEM((4, 1, 128), f32),
             pltpu.VMEM((128, rows), f32),
             pltpu.VMEM((FIELDS, 32, cols + 128), f32),
             pltpu.VMEM((8, cols + 128), f32),
@@ -434,7 +484,7 @@
         ],
         compiler_params=pltpu.CompilerParams(collective_id=0, has_side_effects=True, vmem_limit_bytes=32 * 2**20),
         name="exchange",
-    )(sea_level, transport_u, transport_v, ocean_depth, tracers, land_mask)
+    )(*(pltpu.with_memory_space_constraint(a, pltpu.HBM) for a in arguments))
     return pl.pallas_call(
         functools.partial(store_kernel, len(shapes)),
         out_shape=shapes,
@@ -442,7 +492,7 @@
         out_specs=[anywhere] * 4,
         scratch_shapes=[pltpu.SemaphoreType.DMA((len(shapes),))],
         name="store",
-    )(*held)
+    )(*(pltpu.with_memory_space_constraint(a, pltpu.VMEM) for a in held))
 
 
 MEM = pltpu.VMEM

time: 42.8 us -> 27.6 us (0.64)
  local copies, waits for them, and re-layouts: 9.25 us -> 0 us
  Pallas kernels: 32.5 us -> 26.8 us
    unnamed x20 -> x0, local copies, waits for them, and re-layouts: 9.25 us -> none
    pallas_call x1, Pallas kernels: 29.7 us -> 25.5 us  [local(): pl.pallas_call(exchange_kernel, out_shape=[MEM(s.shape, s.dtype) for s in...]
    pallas_call x1, Pallas kernels: 2.79 us -> 1.31 us  [local(): pl.pallas_call(functools.partial(store_kernel, len(shapes)), out_shape=sh...]
where the time goes in v2:
time: 27.6 us; the launch traced here: 27.5 us
  Pallas kernels  26.8 us (97%)
  between operations  0.64 us (2%)
    pallas_call x1, Pallas kernels, local(): pl.pallas_call(exchange_kernel, out_shape=[MEM(s.shape, s.dtype) for s in...  25.5 us
    pallas_call x1, Pallas kernels, local(): pl.pallas_call(functools.partial(store_kernel, len(shapes)), out_shape=sh...  1.31 us

profile of v2, /device:TPU:1, one launch (start us, length us, event | category | flops | bytes accessed | tf_op | source)
XLA Modules:
  0.0 27.5 jit_solution(7816582787313732299)
XLA Ops:
  0.6 25.5 %exchange.1 = (f32[256,384]{1,0:T(8,128)S(1)}, f32[256,384]{1,0:T(8,128)S(1)}, f32[256,384]{1,0:T(8,128)S(1)}, f32[2,256,384]{2,1,0:T(8,128)S(1)}) custom-call(f32[256,384]{1,0:T(8,128)} %level_in.1, f32[256,384]{1,0:T(8,128)} %u_in.1, f32[256,384]{1,0:T(8,128)} %v_in.1, f32[256,384]{1,0:T(8,128)} %depth_in.1, f32[2,256,384]{2,1,0:T(8,128)} %tracers_in.1, ...), custom_call_target="tpu_custom_call" | custom-call | tf_op jit(solution)/shard_map/exchange/pallas_call | solution.py:462
  26.1 1.3 %store.1 = (f32[256,384]{1,0:T(8,128)}, f32[256,384]{1,0:T(8,128)}, f32[256,384]{1,0:T(8,128)}, f32[2,256,384]{2,1,0:T(8,128)}) custom-call(f32[256,384]{1,0:T(8,128)S(1)} %get-tuple-element.8.refs_0_, f32[256,384]{1,0:T(8,128)S(1)} %get-tuple-element.9.refs_1_, f32[256,384]{1,0:T(8,128)S(1)} %get-tuple-element.10.refs_2_, ...), custom_call_target="tpu_custom_call" | custom-call | tf_op jit(solution)/shard_map/store/pallas_call | solution.py:488

commit v3 on v2

--- a/solution.py
+++ b/solution.py
@@ -200,38 +200,41 @@
         greet(to_w, to_s)
 
     inner = pl.ds(8, rows)
-    loads = [
-        pltpu.make_async_copy(land_in, land, load_sem.at[0]),
-        pltpu.make_async_copy(u_in, x.at[U, inner], load_sem.at[1]),
-        pltpu.make_async_copy(v_in, x.at[V, inner], load_sem.at[2]),
-        pltpu.make_async_copy(level_in, x.at[LEVEL, inner], load_sem.at[3]),
-        pltpu.make_async_copy(depth_in, x.at[DEPTH, inner], load_sem.at[4]),
-        pltpu.make_async_copy(tracers_in, x.at[pl.ds(T0, 2), inner], load_sem.at[5]),
+    arguments = [
+        (u_in, x.at[U, inner]),
+        (v_in, x.at[V, inner]),
+        (level_in, x.at[LEVEL, inner]),
+        (land_in, land),
+        (depth_in, x.at[DEPTH, inner]),
+        (tracers_in, x.at[pl.ds(T0, 2), inner]),
     ]
-    for load in loads:
-        load.start()
+
+    def load(at, k, columns):
+        source, target = arguments[k]
+        where = (slice(None),) * (len(source.shape) - 1) + (columns,)
+        return pltpu.make_async_copy(source.at[where], target.at[where], load_sem.at[at, k])
+
+    ends = (pl.ds(0, 128), pl.ds(cols - 128, 128))
+    end_loads = [[load(at, k, columns) for at, columns in enumerate(ends)] for k in range(len(arguments))]
+    middle = pl.ds(128, cols - 256)
+    middle_loads = [load(2, k, middle) for k in range(len(arguments))] if cols > 256 else []
+    for one in [one for pair in end_loads for one in pair] + middle_loads:
+        one.start()
     for f in range(FIELDS):
         x[f, 0:8] = jnp.ones((8, cols), jnp.float32)
         x[f, rows + 8 : rows + 16] = jnp.ones((8, cols), jnp.float32)
-    for load in loads:
-        load.wait()
-
-    size = 64
-
-    def pack_columns(k, carry):
-        at = pl.multiple_of(k * size, size)
-        x[MASK, pl.ds(at + 8, size)] = land[pl.ds(at, size)].astype(jnp.float32)
-        lane = lanes((size, 128))
-        result = None
-        for f in range(FIELDS):
-            first = x[f, pl.ds(at + 8, size), 0:128]
-            last = x[f, pl.ds(at + 8, size), cols - 128 : cols]
-            ends = roll(jnp.where(lane < 64, first, last), f * GROUP + 8, 1)
-            result = ends if f == 0 else jnp.where(lane < f * GROUP, result, ends)
-        packed[pl.ds(at, size)] = result
-        return carry
-
-    lax.fori_loop(0, rows // size, pack_columns, 0, unroll=True)
+
+    lane = lanes((rows, 128))
+    for f in range(FIELDS):
+        if f != T1:
+            for one in end_loads[f]:
+                one.wait()
+        if f == MASK:
+            first, last = (land[:, columns].astype(jnp.float32) for columns in ends)
+        else:
+            first, last = (x[f, inner, columns] for columns in ends)
+        both = roll(jnp.where(lane < 64, first, last), f * GROUP + 8, 1)
+        packed[...] = both if f == 0 else jnp.where(lane < f * GROUP, packed[...], both)
     packed_t[...] = packed[...].T
 
     groups = [GROUP * f for f in range(FIELDS)]
@@ -242,8 +245,67 @@
     send_corners[SW - SW] = pack_corner(south_end, 0, 8)
     put_columns(send_cols.at[0], pack_last(V, U, [packed_t[g : g + 8] for g in groups]), True)
     put_columns(send_cols.at[1], pack_first(V, U, [packed_t[g + 8 : g + 16] for g in groups]), False)
+
+    def copy(source, target, k, at, to_x, to_y):
+        return pltpu.make_async_remote_copy(
+            src_ref=source,
+            dst_ref=target,
+            send_sem=send_sem.at[k],
+            recv_sem=recv_sem.at[at],
+            device_id=(to_x, to_y),
+            device_id_type=MESH,
+        )
+
+    def corner(k, at, to_x, to_y):
+        return copy(send_corners.at[k - SW], got_corners.at[at - SW], k, at, to_x, to_y)
+
+    away_e = copy(send_cols.at[0], got_cols.at[0], E, W, to_e, me_y)
+    away_w = copy(send_cols.at[1], got_cols.at[1], W, E, to_w, me_y)
+    away_s = copy(send_rows.at[1], got_rows.at[1], S, N, me_x, to_s)
+    away_n = copy(send_rows.at[0], got_rows.at[0], N, S, me_x, to_n)
+    fold_n = copy(send_rows.at[0], got_rows.at[1], N, N, past(me_x), to_n)
+    away_se, away_sw = corner(SE, NW, to_e, to_s), corner(SW, NE, to_w, to_s)
+    away_ne, away_nw = corner(NE, SW, to_e, to_n), corner(NW, SE, to_w, to_n)
+    fold_ne, fold_nw = corner(NE, NE, past(to_e), to_n), corner(NW, NW, past(to_w), to_n)
+    not_top = jnp.logical_not(top)
+    far_ne, far_nw = top & jnp.logical_not(own_ne), top & jnp.logical_not(own_nw)
+
+    count = 3 + jnp.where(own_ne, 0, 1) + jnp.where(own_nw, 0, 1) + jnp.where(has_s, 3, 0)
+    def send_far():
+        @pl.when(not_top)
+        def _():
+            away_ne.start()
+            away_nw.start()
+
+        pl.when(far_ne)(lambda: fold_ne.start())
+        pl.when(far_nw)(lambda: fold_nw.start())
+
+        @pl.when(has_s)
+        def _():
+            away_se.start()
+            away_sw.start()
+
+        away_e.start()
+        away_w.start()
+
+    def send_near():
+        pl.when(not_top)(lambda: away_n.start())
+        pl.when(top)(lambda: fold_n.start())
+        pl.when(has_s)(lambda: away_s.start())
+
+    odd = lax.rem(me_x, 2)
+
+    @pl.when(odd == 1)
+    def _():
+        pl.semaphore_wait(barrier, count)
+        send_far()
+
+    for one in middle_loads:
+        one.wait()
+    x[MASK, inner] = land[...].astype(jnp.float32)
     send_rows[0] = jnp.concatenate(pack_last(U, V, [x[f, rows : rows + 8] for f in range(FIELDS)]), axis=0)
     send_rows[1] = jnp.concatenate(pack_first(U, V, [x[f, 8:16] for f in range(FIELDS)]), axis=0)
+    pl.when(odd == 1)(send_near)
 
     def coriolis(row):
         row = row.astype(jnp.float32)
@@ -264,56 +326,15 @@
         return carry
 
     blocks = rows // BLOCK
-    sends_first = lax.rem(me_x, 2)
-    lax.fori_loop(0, blocks * (1 - sends_first), compute_inner, 0)
-
-    def copy(source, target, k, at, to_x, to_y):
-        return pltpu.make_async_remote_copy(
-            src_ref=source,
-            dst_ref=target,
-            send_sem=send_sem.at[k],
-            recv_sem=recv_sem.at[at],
-            device_id=(to_x, to_y),
-            device_id_type=MESH,
-        )
-
-    def corner(k, at, to_x, to_y):
-        return copy(send_corners.at[k - SW], got_corners.at[at - SW], k, at, to_x, to_y)
-
-    away_e = copy(send_cols.at[0], got_cols.at[0], E, W, to_e, me_y)
-    away_w = copy(send_cols.at[1], got_cols.at[1], W, E, to_w, me_y)
-    away_s = copy(send_rows.at[1], got_rows.at[1], S, N, me_x, to_s)
-    away_n = copy(send_rows.at[0], got_rows.at[0], N, S, me_x, to_n)
-    fold_n = copy(send_rows.at[0], got_rows.at[1], N, N, past(me_x), to_n)
-    away_se, away_sw = corner(SE, NW, to_e, to_s), corner(SW, NE, to_w, to_s)
-    away_ne, away_nw = corner(NE, SW, to_e, to_n), corner(NW, SE, to_w, to_n)
-    fold_ne, fold_nw = corner(NE, NE, past(to_e), to_n), corner(NW, NW, past(to_w), to_n)
-    not_top = jnp.logical_not(top)
-    far_ne, far_nw = top & jnp.logical_not(own_ne), top & jnp.logical_not(own_nw)
-
-    count = 3 + jnp.where(own_ne, 0, 1) + jnp.where(own_nw, 0, 1) + jnp.where(has_s, 3, 0)
-    pl.semaphore_wait(barrier, count)
-
-    @pl.when(not_top)
-    def _():
-        away_n.start()
-        away_ne.start()
-        away_nw.start()
-
-    pl.when(top)(lambda: fold_n.start())
-    pl.when(far_ne)(lambda: fold_ne.start())
-    pl.when(far_nw)(lambda: fold_nw.start())
-
-    @pl.when(has_s)
-    def _():
-        away_s.start()
-        away_se.start()
-        away_sw.start()
-
-    away_e.start()
-    away_w.start()
-
-    lax.fori_loop(blocks * (1 - sends_first), blocks, compute_inner, 0)
+    lax.fori_loop(0, blocks * (1 - odd), compute_inner, 0)
+
+    @pl.when(odd == 0)
+    def _():
+        pl.semaphore_wait(barrier, count)
+        send_near()
+        send_far()
+
+    lax.fori_loop(blocks * (1 - odd), blocks, compute_inner, 0)
 
     away_w.wait_recv()
     away_e.wait_recv()
@@ -354,11 +375,11 @@
     from_ne, from_nw, from_se, from_sw = (got_corners[k - SW] for k in (NE, NW, SE, SW))
     nothing = jnp.zeros((8, 128), jnp.float32)
 
-    @pl.when(not_top)
-    def _():
-        sides = unpack_corner(from_ne, 0, 8, unpack_corner(from_nw, 0, 4, nothing))
-        put_rows(8, unpack_first(U, V, *from_n), sides)
-        other[...] = jnp.zeros_like(other)
+    sides = unpack_corner(from_ne, 0, 8, unpack_corner(from_nw, 0, 4, nothing))
+    put_rows(8, unpack_first(U, V, *from_n), sides)
+    other[...] = jnp.zeros_like(other)
+    sides = unpack_corner(from_se, 4, 8, unpack_corner(from_sw, 4, 4, nothing))
+    put_rows(16, unpack_last(U, V, *from_s), sides)
 
     @pl.when(top)
     def _():
@@ -374,11 +395,6 @@
         mirrored = strip[V, 8:16]
         strip[V, 8:16] = -roll(mirrored, -1, 0)
         other[...] = roll(mirrored, -1, 0)
-
-    @pl.when(has_s)
-    def _():
-        sides = unpack_corner(from_se, 4, 8, unpack_corner(from_sw, 4, 4, nothing))
-        put_rows(16, unpack_last(U, V, *from_s), sides)
 
     @pl.when(bottom)
     def _():
@@ -478,7 +494,7 @@
             pltpu.VMEM((128, rows), f32),
             pltpu.VMEM((FIELDS, 32, cols + 128), f32),
             pltpu.VMEM((8, cols + 128), f32),
-            pltpu.SemaphoreType.DMA((6,)),
+            pltpu.SemaphoreType.DMA((3, 6)),
             pltpu.SemaphoreType.DMA((8,)),
             pltpu.SemaphoreType.DMA((8,)),
         ],

time: 27.6 us -> 27 us (0.978)
  Pallas kernels: 26.8 us -> 26.2 us
    pallas_call x1, Pallas kernels: 25.5 us -> 24.9 us  [local(): pl.pallas_call(exchange_kernel, out_shape=[MEM(s.shape, s.dtype) for s in...]
where the time goes in v3:
time: 27 us; the launch traced here: 26.9 us
  Pallas kernels  26.2 us (97%)
  between operations  0.64 us (2%)
    pallas_call x1, Pallas kernels, local(): pl.pallas_call(exchange_kernel, out_shape=[MEM(s.shape, s.dtype) for s in...  24.9 us
    pallas_call x1, Pallas kernels, local(): pl.pallas_call(functools.partial(store_kernel, len(shapes)), out_shape=sh...  1.31 us

profile of v3, /device:TPU:1, one launch (start us, length us, event | category | flops | bytes accessed | tf_op | source)
XLA Modules:
  0.0 26.9 jit_solution(7211224363857889704)
XLA Ops:
  0.6 24.9 %exchange.1 = (f32[256,384]{1,0:T(8,128)S(1)}, f32[256,384]{1,0:T(8,128)S(1)}, f32[256,384]{1,0:T(8,128)S(1)}, f32[2,256,384]{2,1,0:T(8,128)S(1)}) custom-call(f32[256,384]{1,0:T(8,128)} %level_in.1, f32[256,384]{1,0:T(8,128)} %u_in.1, f32[256,384]{1,0:T(8,128)} %v_in.1, f32[256,384]{1,0:T(8,128)} %depth_in.1, f32[2,256,384]{2,1,0:T(8,128)} %tracers_in.1, ...), custom_call_target="tpu_custom_call" | custom-call | tf_op jit(solution)/shard_map/exchange/pallas_call | solution.py:478
  25.6 1.3 %store.1 = (f32[256,384]{1,0:T(8,128)}, f32[256,384]{1,0:T(8,128)}, f32[256,384]{1,0:T(8,128)}, f32[2,256,384]{2,1,0:T(8,128)}) custom-call(f32[256,384]{1,0:T(8,128)S(1)} %get-tuple-element.8.refs_0_, f32[256,384]{1,0:T(8,128)S(1)} %get-tuple-element.9.refs_1_, f32[256,384]{1,0:T(8,128)S(1)} %get-tuple-element.10.refs_2_, ...), custom_call_target="tpu_custom_call" | custom-call | tf_op jit(solution)/shard_map/store/pallas_call | solution.py:504

commit v4 on v3

--- a/solution.py
+++ b/solution.py
@@ -272,20 +272,13 @@
 
     count = 3 + jnp.where(own_ne, 0, 1) + jnp.where(own_nw, 0, 1) + jnp.where(has_s, 3, 0)
     def send_far():
-        @pl.when(not_top)
-        def _():
-            away_ne.start()
-            away_nw.start()
-
+        pl.when(not_top)(lambda: away_ne.start())
         pl.when(far_ne)(lambda: fold_ne.start())
+        pl.when(has_s)(lambda: away_se.start())
+        away_e.start()
+        pl.when(not_top)(lambda: away_nw.start())
         pl.when(far_nw)(lambda: fold_nw.start())
-
-        @pl.when(has_s)
-        def _():
-            away_se.start()
-            away_sw.start()
-
-        away_e.start()
+        pl.when(has_s)(lambda: away_sw.start())
         away_w.start()
 
     def send_near():
@@ -462,7 +455,7 @@
 
 def store_kernel(count, *refs):
     sems = refs[-1]
-    copies = [pltpu.make_async_copy(refs[k], refs[count + k], sems.at[k]) for k in range(count)]
+    copies = [pltpu.make_async_copy(refs[k], refs[count + k], sems.at[k]) for k in reversed(range(count))]
     for one in copies:
         one.start()
     for one in copies:

time: 27 us -> 27 us (level)
  no operation moved by 1% of the time
where the time goes in v4:
time: 27 us; the launch traced here: 26.9 us
  Pallas kernels  26.2 us (97%)
  between operations  0.64 us (2%)
    pallas_call x1, Pallas kernels, local(): pl.pallas_call(exchange_kernel, out_shape=[MEM(s.shape, s.dtype) for s in...  24.9 us
    pallas_call x1, Pallas kernels, local(): pl.pallas_call(functools.partial(store_kernel, len(shapes)), out_shape=sh...  1.3 us

profile of v4, /device:TPU:1, one launch (start us, length us, event | category | flops | bytes accessed | tf_op | source)
XLA Modules:
  0.0 26.9 jit_solution(8107047253576111140)
XLA Ops:
  0.6 24.9 %exchange.1 = (f32[256,384]{1,0:T(8,128)S(1)}, f32[256,384]{1,0:T(8,128)S(1)}, f32[256,384]{1,0:T(8,128)S(1)}, f32[2,256,384]{2,1,0:T(8,128)S(1)}) custom-call(f32[256,384]{1,0:T(8,128)} %level_in.1, f32[256,384]{1,0:T(8,128)} %u_in.1, f32[256,384]{1,0:T(8,128)} %v_in.1, f32[256,384]{1,0:T(8,128)} %depth_in.1, f32[2,256,384]{2,1,0:T(8,128)} %tracers_in.1, ...), custom_call_target="tpu_custom_call" | custom-call | tf_op jit(solution)/shard_map/exchange/pallas_call | solution.py:471
  25.6 1.3 %store.1 = (f32[256,384]{1,0:T(8,128)}, f32[256,384]{1,0:T(8,128)}, f32[256,384]{1,0:T(8,128)}, f32[2,256,384]{2,1,0:T(8,128)}) custom-call(f32[256,384]{1,0:T(8,128)S(1)} %get-tuple-element.8.refs_0_, f32[256,384]{1,0:T(8,128)S(1)} %get-tuple-element.9.refs_1_, f32[256,384]{1,0:T(8,128)S(1)} %get-tuple-element.10.refs_2_, ...), custom_call_target="tpu_custom_call" | custom-call | tf_op jit(solution)/shard_map/store/pallas_call | solution.py:497
